TPU v7x, 512 devices: a whole 4x8x8 slice. The times are simulated.
512 devices in a mesh: lat: 16 (over y, z_lo), lon: 32 (over z_hi, x, core).
Axes of the slice: x: 4, y: 8, z: 8 (z_hi: 4, z_lo: 2; z = z_hi * 2 + z_lo), core: 2. Of those that a mesh axis runs over, the one named last changes fastest.
Arguments:
- fields: bfloat16 [384, 512, 192], P('lat', 'lon'), may hold values from -6 to 6
- first_weight: bfloat16 [3, 3, 192, 192], replicated, may hold values from -0.15625 to 0.15625
- first_gamma: float32 [192, 192], replicated, may hold values from 0 to 0.010416667
- first_beta: float32 [192], replicated, may hold values from 0.5 to 2
- second_weight: bfloat16 [3, 3, 192, 192], replicated, may hold values from -0.15625 to 0.15625
- second_gamma: float32 [192, 192], replicated, may hold values from 0 to 0.010416667
- second_beta: float32 [192], replicated, may hold values from 0.5 to 2
- cotangent: bfloat16 [384, 512, 192], P('lat', 'lon'), may hold values from -0.015625 to 0.015625
Outputs:
- encoded: bfloat16 [384, 512, 192], P('lat', 'lon')
- first_wgrad: bfloat16 [3, 3, 192, 192], replicated
- first_ggrad: float32 [192, 192], replicated
- first_bgrad: float32 [192], replicated
- second_wgrad: bfloat16 [3, 3, 192, 192], replicated
- second_ggrad: float32 [192, 192], replicated
- second_bgrad: float32 [192], replicated
All inputs are finite; a program needn't handle non-finite values.
Results may differ from a plain program's by a relative error of at most 0.007.
Values may be sent and summed in bfloat16 or wider, within the bound.
A program may use at most 64 MiB of HBM per device.

v0:
```python
import jax
import jax.numpy as jnp
from jax import lax
from jax.sharding import PartitionSpec as P


def padded_2(block, sides, width, periodic):
    for axis, dim in sides:
        count = lax.axis_size(axis)
        forward = [(i, i + 1) for i in range(count - 1)]
        if periodic:
            forward.append((count - 1, 0))
        backward = [(target, source) for source, target in forward]
        low = lax.ppermute(
            lax.slice_in_dim(block, block.shape[dim] - width, None, axis=dim), axis, forward
        )
        high = lax.ppermute(lax.slice_in_dim(block, 0, width, axis=dim), axis, backward)
        block = jnp.concatenate([low, block, high], axis=dim)
    return block


def from_behind(block, axis, distance):
    devices = range(lax.axis_size(axis))
    route = [((i - distance) % len(devices), i) for i in devices]
    return lax.ppermute(block, axis, route)


def border(field):
    half = lax.axis_size("lon") // 2
    last_band = lax.axis_size("lat") - 1
    band = lax.axis_index("lat")
    rows = padded_2(field, (("lat", 0),), 1, False)
    edges = jnp.stack([field[0], field[-1]])
    folded = from_behind(edges, "lon", half)
    top_row = jnp.where(band == 0, folded[0], rows[0])
    bottom_row = jnp.where(band == last_band, folded[1], rows[-1])
    rows = jnp.concatenate([top_row[None], rows[1:-1], bottom_row[None]], axis=0)
    return padded_2(rows, (("lon", 1),), 1, True)


def unborder(grad):
    half = lax.axis_size("lon") // 2
    last_band = lax.axis_size("lat") - 1
    band = lax.axis_index("lat")
    sides = jnp.stack([grad[:, 0], grad[:, -1]], axis=1)
    arrived = padded_2(sides.astype(jnp.bfloat16), (("lon", 1),), 1, True).astype(sides.dtype)
    rows = grad[:, 1:-1]
    rows = rows.at[:, 0].add(arrived[:, 0]).at[:, -1].add(arrived[:, -1])
    edges = jnp.stack([rows[0], rows[-1]])
    returned = from_behind(edges, "lon", half)
    across = padded_2(edges, (("lat", 0),), 1, False)
    top_add = jnp.where(band == 0, returned[0], across[0])
    bottom_add = jnp.where(band == last_band, returned[1], across[-1])
    inner = rows[1:-1]
    inner = inner.at[0].add(top_add)
    inner = inner.at[-1].add(bottom_add)
    return inner


def convolve(padded, weight):
    rows_n = padded.shape[0] - 2
    cols_n = padded.shape[1] - 2
    chans = padded.shape[2]
    total = jnp.zeros((rows_n * cols_n, weight.shape[3]), jnp.float32)
    for row_off in range(3):
        for col_off in range(3):
            window = padded[row_off : row_off + rows_n, col_off : col_off + cols_n].reshape(
                -1, chans
            )
            total = total + jnp.dot(
                window, weight[row_off, col_off], preferred_element_type=jnp.float32
            )
    return total.reshape(rows_n, cols_n, -1)


def spread(grad, weight):
    rows_n, cols_n, outs_n = grad.shape
    flat = grad.reshape(-1, outs_n)
    total = jnp.zeros((rows_n + 2, cols_n + 2, weight.shape[2]), jnp.float32)
    for row_off in range(3):
        for col_off in range(3):
            term = lax.dot_general(
                flat,
                weight[row_off, col_off],
                (((1,), (1,)), ((), ())),
                preferred_element_type=jnp.float32,
            )
            term = term.reshape(rows_n, cols_n, -1)
            total = total + jnp.pad(term, ((row_off, 2 - row_off), (col_off, 2 - col_off), (0, 0)))
    return total


def weight_grad(padded, grad):
    rows_n, cols_n, outs_n = grad.shape
    chans = padded.shape[2]
    flat = grad.reshape(-1, outs_n)
    pieces = []
    for row_off in range(3):
        for col_off in range(3):
            window = padded[row_off : row_off + rows_n, col_off : col_off + cols_n].reshape(
                -1, chans
            )
            pieces.append(
                lax.dot_general(
                    window, flat, (((0,), (0,)), ((), ())), preferred_element_type=jnp.float32
                )
            )
    return jnp.stack(pieces).reshape(3, 3, chans, outs_n)


def normalize(z, gamma, beta):
    chans = z.shape[2]
    sq = z * z
    summed = lax.dot_general(
        sq.reshape(-1, chans), gamma, (((1,), (1,)), ((), ())), precision=lax.Precision.HIGHEST
    )
    scale = lax.rsqrt(beta + summed.reshape(z.shape))
    return (z * scale, scale, sq)


def denormalize(upper, z, scale, sq, gamma):
    chans = z.shape[2]
    lever = upper * z * scale * scale * scale
    flat = lever.reshape(-1, chans)
    mixed = jnp.dot(flat, gamma, precision=lax.Precision.HIGHEST).reshape(z.shape)
    lower = upper * scale - z * mixed
    gamma_grad = -0.5 * lax.dot_general(
        flat, sq.reshape(-1, chans), (((0,), (0,)), ((), ())), precision=lax.Precision.HIGHEST
    )
    beta_grad = -0.5 * jnp.sum(flat, axis=0)
    return (lower, gamma_grad, beta_grad)


def combine_grads(wgrad, ggrad, bgrad):
    wsum, gsum, bsum = lax.psum((wgrad, ggrad, bgrad), ("lat", "lon"))
    return (wsum.astype(jnp.bfloat16), gsum, bsum)


def per_device(
    fields,
    first_weight,
    first_gamma,
    first_beta,
    second_weight,
    second_gamma,
    second_beta,
    cotangent,
):
    padded_x = border(fields)
    z_first = convolve(padded_x, first_weight)
    h_first, scale_one, sq_one = normalize(z_first, first_gamma, first_beta)
    hidden = h_first.astype(jnp.bfloat16)
    padded_h = border(hidden)
    z_second = convolve(padded_h, second_weight)
    out_float, scale_two, sq_two = normalize(z_second, second_gamma, second_beta)
    encoded = out_float.astype(jnp.bfloat16)
    dz_two, ggrad_two, bgrad_two = denormalize(
        cotangent.astype(jnp.float32), z_second, scale_two, sq_two, second_gamma
    )
    grad_two = dz_two.astype(jnp.bfloat16)
    wgrad_two = weight_grad(padded_h, grad_two)
    wgrad_two, ggrad_two, bgrad_two = combine_grads(wgrad_two, ggrad_two, bgrad_two)
    dhidden = unborder(spread(grad_two, second_weight))
    dz_one, ggrad_one, bgrad_one = denormalize(dhidden, z_first, scale_one, sq_one, first_gamma)
    grad_one = dz_one.astype(jnp.bfloat16)
    wgrad_one = weight_grad(padded_x, grad_one)
    wgrad_one, ggrad_one, bgrad_one = combine_grads(wgrad_one, ggrad_one, bgrad_one)
    return (encoded, wgrad_one, ggrad_one, bgrad_one, wgrad_two, ggrad_two, bgrad_two)


def solution(mesh):
    return jax.shard_map(
        per_device,
        mesh=mesh,
        in_specs=(P("lat", "lon", None), P(), P(), P(), P(), P(), P(), P("lat", "lon", None)),
        out_specs=(P("lat", "lon", None), P(), P(), P(), P(), P(), P()),
        check_vma=False,
    )
```

profile of v0, /device:TPU:1, one launch (start us, length us, event | category | flops | bytes accessed | tf_op | source)
XLA Modules:
  0.0 400.7 jit_solution(5051696582323135277)
XLA Ops:
  8.0 11.5 %collective-permute-start = (bf16[2,16,192]{2,1,0:T(8,128)(2,1)S(1)}, bf16[2,16,192]{2,1,0:T(8,128)(2,1)S(1)}, u32[]{:S(2)}, u32[]{:S(2)}) collective-permute-start(bf16[2,16,192]{2,1,0:T(8,128)(2,1)S(1)} %pad_maximum_fusion.16), channel_id=1, source_target_pairs={{16,0},{17,1},{18,2},{19,3},{20,4},{21,5},{22,6},{23,7},{24,8},{25... | collective-permute-start | bytes 36872 | tf_op jit(solution)/shard_map/ppermute | solution.py:25
  19.5 3.1 collective-permute-start.1
  22.6 1.3 collective-permute-start.2
  24.9 2.1 collective-permute-done.2
  27.0 4.3 %collective-permute-start.4 = (bf16[26,1,192]{2,0,1:T(8,128)(2,1)S(1)}, bf16[26,1,192]{2,0,1:T(8,128)(2,1)S(1)}, u32[]{:S(2)}, u32[]{:S(2)}) collective-permute-start(bf16[26,1,192]{2,0,1:T(8,128)(2,1)S(1)} %get-tuple-element.83), channel_id=1, source_target_pairs={{1,0},{2,1},{3,2},{4,3},{5,4},{6,5},{7,6},{8,7},{9,8},{10,9},{11,1... | collective-permute-start | bytes 29960 | tf_op jit(solution)/shard_map/ppermute | solution.py:17
  31.3 3.0 collective-permute-start.3
  40.2 6.2 %collective-permute-start.5 = (bf16[2,16,192]{2,1,0:T(8,128)(2,1)S(1)}, bf16[2,16,192]{2,1,0:T(8,128)(2,1)S(1)}, u32[]{:S(2)}, u32[]{:S(2)}) collective-permute-start(bf16[2,16,192]{2,1,0:T(8,128)(2,1)S(1)} %pad_maximum_fusion.17), channel_id=1, source_target_pairs={{16,0},{17,1},{18,2},{19,3},{20,4},{21,5},{22,6},{23,7},{24,8},{25... | collective-permute-start | bytes 36872 | tf_op jit(solution)/shard_map/ppermute | solution.py:25
  46.4 1.3 collective-permute-start.7
  47.7 4.7 %collective-permute-start.6 = (bf16[1,16,192]{2,1,0:T(8,128)(2,1)S(1)}, bf16[1,16,192]{2,1,0:T(8,128)(2,1)S(1)}, u32[]{:S(2)}, u32[]{:S(2)}) collective-permute-start(bf16[1,16,192]{2,1,0:T(8,128)(2,1)S(1)} %get-tuple-element.92), channel_id=1, source_target_pairs={{0,32},{32,64},{64,96},{96,128},{128,160},{160,192},{192,224},{224... | collective-permute-start | bytes 18440 | tf_op jit(solution)/shard_map/ppermute | solution.py:14
  53.3 9.7 %collective-permute-start.9 = (bf16[26,1,192]{2,1,0:T(2,128)(2,1)S(1)}, bf16[26,1,192]{2,1,0:T(2,128)(2,1)S(1)}, u32[]{:S(2)}, u32[]{:S(2)}) collective-permute-start(bf16[26,1,192]{2,1,0:T(2,128)(2,1)S(1)} %get-tuple-element.87), channel_id=1, source_target_pairs={{1,0},{2,1},{3,2},{4,3},{5,4},{6,5},{7,6},{8,7},{9,8},{10,9},{11,1... | collective-permute-start | bytes 29960 | tf_op jit(solution)/shard_map/ppermute | solution.py:17
  63.1 1.9 collective-permute-start.8
  71.4 2.3 fusion.38
  74.3 1.5 fusion.6
  78.9 4.0 collective-permute-start.10
  82.9 6.1 %collective-permute-start.11 = (bf16[26,1,192]{2,1,0:T(2,128)(2,1)S(1)}, bf16[26,1,192]{2,1,0:T(2,128)(2,1)S(1)}, u32[]{:S(2)}, u32[]{:S(2)}) collective-permute-start(bf16[26,1,192]{2,1,0:T(2,128)(2,1)S(1)} %get-tuple-element.68), channel_id=1, source_target_pairs={{1,0},{2,1},{3,2},{4,3},{5,4},{6,5},{7,6},{8,7},{9,8},{10,9},{11,1... | collective-permute-start | bytes 29960 | tf_op jit(solution)/shard_map/ppermute | solution.py:17
  92.9 4.5 %collective-permute-start.13 = (f32[1,16,192]{2,1,0:T(8,128)S(1)}, f32[1,16,192]{2,1,0:T(8,128)S(1)}, u32[]{:S(2)}, u32[]{:S(2)}) collective-permute-start(f32[1,16,192]{2,1,0:T(8,128)S(1)} %get-tuple-element.66), channel_id=1, source_target_pairs={{0,32},{32,64},{64,96},{96,128},{128,160},{160,192},{192,224},{224... | collective-permute-start | bytes 36872 | tf_op jit(solution)/shard_map/ppermute | solution.py:14
  97.5 2.1 collective-permute-start.12
  99.6 1.3 collective-permute-start.14
  101.0 5.1 %collective-permute-done.12 = f32[2,16,192]{2,1,0:T(8,128)S(1)} collective-permute-done((f32[2,16,192]{2,1,0:T(8,128)S(1)}, f32[2,16,192]{2,1,0:T(8,128)S(1)}, u32[]{:S(2)}, u32[]{:S(2)}) %collective-permute-start.12) | collective-permute-done | bytes 24608 | tf_op jit(solution)/shard_map/ppermute | solution.py:25
  106.8 1.5 fusion.14
  112.0 126.0 %all-reduce.15 = (bf16[3,3,192,192]{3,2,1,0:T(8,128)(2,1)}, f32[192]{0:T(256)}, bf16[3,3,192,192]{3,2,1,0:T(8,128)(2,1)}, f32[192]{0:T(256)}) all-reduce(f32[3,3,192,192]{3,2,1,0:T(8,128)} %bitcast.288, f32[192]{0:T(256)S(1)} %broadcast_multiply_fusion.1, ...), channel_id=1, replica_groups=mesh['lat'=16,'lon'=32] {'lat','lon'}, use_global_device_ids=true, to_apply=%region_0.1 | all-reduce | flops 663936 | bytes 3984384 | tf_op jit(solution)/shard_map/psum | solution.py:135
  238.0 152.6 %all-reduce.14.cloned.1.call-done = (f32[192,192]{1,0:T(8,128)}, f32[192,192]{1,0:T(8,128)}) async-done(((f32[192,192]{1,0:T(8,128)}, f32[192,192]{1,0:T(8,128)}), (f32[192,192]{1,0:T(8,128)}, f32[192,192]{1,0:T(8,128)})) %all-reduce.14.cloned.1.call-update) | async-done | bytes 294928 | tf_op jit(solution)/shard_map/psum | solution.py:135
  390.6 1.6 copy.187
  392.2 1.6 copy.188
  (144 shorter events, 26.2 us)
Async XLA Ops:
  7.2 64.2 %copy-start = (f32[192,192]{1,0:T(8,128)S(1)}, f32[192,192]{1,0:T(8,128)}, u32[]{:S(2)}) copy-start(f32[192,192]{1,0:T(8,128)} %param.21) | copy-start | bytes 442372
  7.2 383.4 %all-reduce.14.cloned.1.call-start = ((), (), s32[]{:S(2)}) async-start(), calls=%async_computation | async-start | bytes 786432 | tf_op jit(solution)/shard_map/psum | solution.py:135
  8.0 19.0 %collective-permute-start = (bf16[2,16,192]{2,1,0:T(8,128)(2,1)S(1)}, bf16[2,16,192]{2,1,0:T(8,128)(2,1)S(1)}, u32[]{:S(2)}, u32[]{:S(2)}) collective-permute-start(bf16[2,16,192]{2,1,0:T(8,128)(2,1)S(1)} %pad_maximum_fusion.16), channel_id=1, source_target_pairs={{16,0},{17,1},{18,2},{19,3},{20,4},{21,5},{22,6},{23,7},{24,8},{25... | collective-permute-start | bytes 36872 | tf_op jit(solution)/shard_map/ppermute | solution.py:25
  19.5 5.4 %collective-permute-start.1 = (bf16[1,16,192]{2,1,0:T(8,128)(2,1)S(1)}, bf16[1,16,192]{2,1,0:T(8,128)(2,1)S(1)}, u32[]{:S(2)}, u32[]{:S(2)}) collective-permute-start(bf16[1,16,192]{2,1,0:T(8,128)(2,1)S(1)} %get-tuple-element.95), channel_id=1, source_target_pairs={{0,32},{32,64},{64,96},{96,128},{128,160},{160,192},{192,224},{224... | collective-permute-start | bytes 18440 | tf_op jit(solution)/shard_map/ppermute | solution.py:14
  22.6 4.4 %collective-permute-start.2 = (bf16[1,16,192]{2,1,0:T(8,128)(2,1)S(1)}, bf16[1,16,192]{2,1,0:T(8,128)(2,1)S(1)}, u32[]{:S(2)}, u32[]{:S(2)}) collective-permute-start(bf16[1,16,192]{2,1,0:T(8,128)(2,1)S(1)} %get-tuple-element.96), channel_id=1, source_target_pairs={{32,0},{64,32},{96,64},{128,96},{160,128},{192,160},{224,192},{256... | collective-permute-start | bytes 18440 | tf_op jit(solution)/shard_map/ppermute | solution.py:17
  27.0 7.6 %collective-permute-start.4 = (bf16[26,1,192]{2,0,1:T(8,128)(2,1)S(1)}, bf16[26,1,192]{2,0,1:T(8,128)(2,1)S(1)}, u32[]{:S(2)}, u32[]{:S(2)}) collective-permute-start(bf16[26,1,192]{2,0,1:T(8,128)(2,1)S(1)} %get-tuple-element.83), channel_id=1, source_target_pairs={{1,0},{2,1},{3,2},{4,3},{5,4},{6,5},{7,6},{8,7},{9,8},{10,9},{11,1... | collective-permute-start | bytes 29960 | tf_op jit(solution)/shard_map/ppermute | solution.py:17
  31.3 3.9 collective-permute-start.3
  35.9 2.0 copy-start.4
  39.4 25.6 %copy-start.1 = (bf16[3,3,192,192]{3,2,1,0:T(8,128)(2,1)S(1)}, bf16[3,3,192,192]{3,2,1,0:T(8,128)(2,1)}, u32[]{:S(2)}) copy-start(bf16[3,3,192,192]{3,2,1,0:T(8,128)(2,1)} %param.20) | copy-start | bytes 1990660
  40.2 13.0 %collective-permute-start.5 = (bf16[2,16,192]{2,1,0:T(8,128)(2,1)S(1)}, bf16[2,16,192]{2,1,0:T(8,128)(2,1)S(1)}, u32[]{:S(2)}, u32[]{:S(2)}) collective-permute-start(bf16[2,16,192]{2,1,0:T(8,128)(2,1)S(1)} %pad_maximum_fusion.17), channel_id=1, source_target_pairs={{16,0},{17,1},{18,2},{19,3},{20,4},{21,5},{22,6},{23,7},{24,8},{25... | collective-permute-start | bytes 36872 | tf_op jit(solution)/shard_map/ppermute | solution.py:25
  46.4 6.0 %collective-permute-start.7 = (bf16[1,16,192]{2,1,0:T(8,128)(2,1)S(1)}, bf16[1,16,192]{2,1,0:T(8,128)(2,1)S(1)}, u32[]{:S(2)}, u32[]{:S(2)}) collective-permute-start(bf16[1,16,192]{2,1,0:T(8,128)(2,1)S(1)} %get-tuple-element.91), channel_id=1, source_target_pairs={{32,0},{64,32},{96,64},{128,96},{160,128},{192,160},{224,192},{256... | collective-permute-start | bytes 18440 | tf_op jit(solution)/shard_map/ppermute | solution.py:17
  47.7 5.5 %collective-permute-start.6 = (bf16[1,16,192]{2,1,0:T(8,128)(2,1)S(1)}, bf16[1,16,192]{2,1,0:T(8,128)(2,1)S(1)}, u32[]{:S(2)}, u32[]{:S(2)}) collective-permute-start(bf16[1,16,192]{2,1,0:T(8,128)(2,1)S(1)} %get-tuple-element.92), channel_id=1, source_target_pairs={{0,32},{32,64},{64,96},{96,128},{128,160},{160,192},{192,224},{224... | collective-permute-start | bytes 18440 | tf_op jit(solution)/shard_map/ppermute | solution.py:14
  53.3 11.9 %collective-permute-start.9 = (bf16[26,1,192]{2,1,0:T(2,128)(2,1)S(1)}, bf16[26,1,192]{2,1,0:T(2,128)(2,1)S(1)}, u32[]{:S(2)}, u32[]{:S(2)}) collective-permute-start(bf16[26,1,192]{2,1,0:T(2,128)(2,1)S(1)} %get-tuple-element.87), channel_id=1, source_target_pairs={{1,0},{2,1},{3,2},{4,3},{5,4},{6,5},{7,6},{8,7},{9,8},{10,9},{11,1... | collective-permute-start | bytes 29960 | tf_op jit(solution)/shard_map/ppermute | solution.py:17
  63.1 3.1 collective-permute-start.8
  68.1 3.3 copy-start.16
  71.4 2.4 copy-start.15
  78.9 12.3 %collective-permute-start.10 = (bf16[26,1,192]{2,1,0:T(2,128)(2,1)S(1)}, bf16[26,1,192]{2,1,0:T(2,128)(2,1)S(1)}, u32[]{:S(2)}, u32[]{:S(2)}) collective-permute-start(bf16[26,1,192]{2,1,0:T(2,128)(2,1)S(1)} %get-tuple-element.67), channel_id=1, source_target_pairs={{0,1},{1,2},{2,3},{3,4},{4,5},{5,6},{6,7},{7,8},{8,9},{9,10},{10,1... | collective-permute-start | bytes 29960 | tf_op jit(solution)/shard_map/ppermute | solution.py:14
  82.9 8.3 %collective-permute-start.11 = (bf16[26,1,192]{2,1,0:T(2,128)(2,1)S(1)}, bf16[26,1,192]{2,1,0:T(2,128)(2,1)S(1)}, u32[]{:S(2)}, u32[]{:S(2)}) collective-permute-start(bf16[26,1,192]{2,1,0:T(2,128)(2,1)S(1)} %get-tuple-element.68), channel_id=1, source_target_pairs={{1,0},{2,1},{3,2},{4,3},{5,4},{6,5},{7,6},{8,7},{9,8},{10,9},{11,1... | collective-permute-start | bytes 29960 | tf_op jit(solution)/shard_map/ppermute | solution.py:17
  91.1 15.2 %copy-start.14 = (f32[192,192]{1,0:T(8,128)S(1)}, f32[192,192]{1,0:T(8,128)}, u32[]{:S(2)}) copy-start(f32[192,192]{1,0:T(8,128)} %param.18) | copy-start | bytes 442372
  92.9 8.0 %collective-permute-start.13 = (f32[1,16,192]{2,1,0:T(8,128)S(1)}, f32[1,16,192]{2,1,0:T(8,128)S(1)}, u32[]{:S(2)}, u32[]{:S(2)}) collective-permute-start(f32[1,16,192]{2,1,0:T(8,128)S(1)} %get-tuple-element.66), channel_id=1, source_target_pairs={{0,32},{32,64},{64,96},{96,128},{128,160},{160,192},{192,224},{224... | collective-permute-start | bytes 36872 | tf_op jit(solution)/shard_map/ppermute | solution.py:14
  97.5 8.6 %collective-permute-start.12 = (f32[2,16,192]{2,1,0:T(8,128)S(1)}, f32[2,16,192]{2,1,0:T(8,128)S(1)}, u32[]{:S(2)}, u32[]{:S(2)}) collective-permute-start(f32[2,16,192]{2,1,0:T(8,128)S(1)} %pad_maximum_fusion.6), channel_id=1, source_target_pairs={{16,0},{17,1},{18,2},{19,3},{20,4},{21,5},{22,6},{23,7},{24,8},{25... | collective-permute-start | bytes 73736 | tf_op jit(solution)/shard_map/ppermute | solution.py:25
  99.6 6.5 %collective-permute-start.14 = (f32[1,16,192]{2,1,0:T(8,128)S(1)}, f32[1,16,192]{2,1,0:T(8,128)S(1)}, u32[]{:S(2)}, u32[]{:S(2)}) collective-permute-start(f32[1,16,192]{2,1,0:T(8,128)S(1)} %get-tuple-element.65), channel_id=1, source_target_pairs={{32,0},{64,32},{96,64},{128,96},{160,128},{192,160},{224,192},{256... | collective-permute-start | bytes 36872 | tf_op jit(solution)/shard_map/ppermute | solution.py:17
  106.7 1.8 copy-start.12
  110.2 1.7 copy-start.6
  (10 other events, 10.6 us)
Sparse Core Ops, SparseCore 0:
  112.1 278.4 all-reduce.13
where the time goes:
time: 401 us
  waiting for transfers between devices  162 us (40%)
  blocking collectives  126 us (31%)
  starting transfers between devices  65.2 us (16%)
  matrix products  18.7 us (5%)
  between operations  15 us (4%)
  local copies, waits for them, and re-layouts  12 us (3%)
    psum x1, waiting for transfers between devices, combine_grads(): wsum, gsum, bsum = lax.psum((wgrad, ggrad, bgrad), ('lat', 'lon'))  153 us
    psum x1, blocking collectives, combine_grads(): wsum, gsum, bsum = lax.psum((wgrad, ggrad, bgrad), ('lat', 'lon'))  126 us
    ppermute x6, starting transfers between devices, padded_2(): lax.ppermute(lax.slice_in_dim(block, 0, width, axis=dim), axis, backward)  24 us
    ppermute x6, starting transfers between devices, padded_2(): lax.ppermute(lax.slice_in_dim(block, block.shape[dim] - width, None, axis...  21.3 us
    ppermute x3, starting transfers between devices, from_behind(): return lax.ppermute(block, axis, route)  19.8 us
  transfers between devices with their start and end apart: 16, of which 6 were waited for; matrix products, arithmetic and copies ran while one was open for 1% of the time, Pallas kernels for 0%

commit v1 on v0

--- a/solution.py
+++ b/solution.py
@@ -1,9 +1,294 @@
+import functools
+
 import jax
 import jax.numpy as jnp
 from jax import lax
+from jax.experimental import pallas as pl
+from jax.experimental.pallas import tpu as pltpu
 from jax.sharding import PartitionSpec as P
 
-
+MESH = pl.DeviceIdType.MESH
+BF16 = jnp.bfloat16
+F32 = jnp.float32
+NX, NY, NZ = 4, 8, 8
+ROWS = 3072
+HALF = ROWS // 2
+PART = HALF // NX
+SHARD = PART // NY
+SLOTS = 32
+
+
+def coordinates():
+    lat, lon = lax.axis_index("lat"), lax.axis_index("lon")
+    core = lax.rem(lon, 2)
+    x = lax.rem(lax.div(lon, 2), NX)
+    z = lax.div(lon, 2 * NX) * 2 + lax.rem(lat, 2)
+    y = lax.div(lat, 2)
+    return core, x, y, z
+
+
+def at(core, x, y, z):
+    return (y * 2 + lax.rem(z, 2), lax.div(z, 2) * (2 * NX) + x * 2 + core)
+
+
+def partners():
+    core, x, y, z = coordinates()
+    found = [at(1 - core, x, y, z)]
+    found += [at(core, lax.rem(x + d, NX), y, z) for d in range(1, NX)]
+    found += [at(core, x, lax.rem(y + d, NY), z) for d in range(1, NY)]
+    found += [at(core, x, y, lax.rem(z + d, NZ)) for d in range(1, NZ)]
+    return found
+
+
+class Reduction:
+    def __init__(self, layer, grads, core_out, core_in, x_out, x_in, y_out, y_in, z_in, y_all, full, sums, send, recv):
+        self.layer = layer
+        self.grads, self.full = grads, full
+        self.core_out, self.core_in = core_out, core_in
+        self.x_out, self.x_in = x_out, x_in
+        self.y_out, self.y_in = y_out, y_in
+        self.z_in, self.y_all = z_in, y_all
+        self.sums = sums
+        self.send, self.recv = send, recv
+        self.me = coordinates()
+
+    def copy(self, source, target, slot, device):
+        made = pltpu.make_async_remote_copy(
+            src_ref=source,
+            dst_ref=target,
+            send_sem=self.send.at[self.layer, slot],
+            recv_sem=self.recv.at[self.layer, slot],
+            device_id=device,
+            device_id_type=MESH,
+        )
+        return made
+
+    def core_copy(self):
+        core, x, y, z = self.me
+        return self.copy(self.core_out, self.core_in, 0, at(1 - core, x, y, z))
+
+    def x_copy(self, d):
+        core, x, y, z = self.me
+        return self.copy(self.x_out.at[d - 1], self.x_in.at[d - 1], d, at(core, lax.rem(x + d, NX), y, z))
+
+    def y_copy(self, d):
+        core, x, y, z = self.me
+        return self.copy(self.y_out.at[d - 1], self.y_in.at[d - 1], 3 + d, at(core, x, lax.rem(y + d, NY), z))
+
+    def z_copy(self, d):
+        core, x, y, z = self.me
+        return self.copy(self.z_in.at[z], self.z_in.at[z], 10 + d, at(core, x, y, lax.rem(z + d, NZ)))
+
+    def z_arrival(self, d):
+        core, x, y, z = self.me
+        other = lax.rem(z + NZ - d, NZ)
+        return self.copy(self.z_in.at[other], self.z_in.at[other], 10 + d, at(core, x, y, other))
+
+    def y_gather(self, d, arrival=False):
+        core, x, y, z = self.me
+        row = lax.rem(y + NY - d, NY) if arrival else y
+        ref = self.y_all.at[row]
+        return self.copy(ref, ref, 17 + d, at(core, x, lax.rem(y + d, NY), z))
+
+    def part(self, core, x):
+        return self.full.at[core, x]
+
+    def x_gather(self, d, arrival=False):
+        core, x, y, z = self.me
+        ref = self.part(core, lax.rem(x + NX - d, NX) if arrival else x)
+        return self.copy(ref, ref, 24 + d, at(core, lax.rem(x + d, NX), y, z))
+
+    def core_gather(self, d, arrival=False):
+        core, x, y, z = self.me
+        ref = self.part(1 - core if arrival else core, lax.rem(x + NX - d, NX))
+        return self.copy(ref, ref, 28 + d, at(1 - core, x, y, z))
+
+    def start_core(self):
+        core, x, y, z = self.me
+        self.core_out[...] = self.grads[1 - core].astype(BF16)
+        self.core_copy().start()
+
+    def core_to_x(self):
+        core, x, y, z = self.me
+        self.core_copy().wait_recv()
+        for d in range(1, NX):
+            other = lax.rem(x + d, NX)
+            self.x_out[d - 1] = (self.grads[core, other] + self.core_in[other].astype(F32)).astype(BF16)
+            self.x_copy(d).start()
+        own = self.grads[core, x] + self.core_in[x].astype(F32)
+        self.sums[...] = own.reshape(self.sums.shape)
+
+    def x_to_y(self):
+        core, x, y, z = self.me
+        total = self.sums[...]
+        for d in range(1, NX):
+            self.x_copy(d).wait_recv()
+            total = total + self.x_in[d - 1].astype(F32).reshape(total.shape)
+        self.sums[...] = total
+        for d in range(1, NY):
+            self.y_out[d - 1] = self.sums[lax.rem(y + d, NY)].astype(BF16)
+            self.y_copy(d).start()
+
+    def y_to_z(self):
+        core, x, y, z = self.me
+        total = self.sums[y]
+        for d in range(1, NY):
+            self.y_copy(d).wait_recv()
+            total = total + self.y_in[d - 1].astype(F32)
+        self.z_in[z] = total.astype(BF16)
+        for d in range(1, NZ):
+            self.z_copy(d).start()
+
+    def z_to_y(self):
+        core, x, y, z = self.me
+        for d in range(1, NZ):
+            self.z_arrival(d).wait_recv()
+        total = self.z_in[0].astype(F32)
+        for place in range(1, NZ):
+            total = total + self.z_in[place].astype(F32)
+        self.y_all[y] = total.astype(BF16)
+        for d in range(1, NY):
+            self.y_gather(d).start()
+
+    def y_to_x(self):
+        core, x, y, z = self.me
+        for d in range(1, NY):
+            self.y_gather(d, arrival=True).wait_recv()
+        whole = self.y_all[...].astype(F32).reshape(PART, 128)
+        for block in range(PART // 128):
+            turned = whole[block * 128 : (block + 1) * 128].T
+            self.full[core, x, block * 128 : (block + 1) * 128] = turned.astype(BF16)
+        for d in range(1, NX):
+            self.x_gather(d).start()
+        self.core_gather(0).start()
+
+    def x_to_core(self):
+        for d in range(1, NX):
+            self.x_gather(d, arrival=True).wait_recv()
+            self.core_gather(d).start()
+
+    def core_done(self):
+        for d in range(NX):
+            self.core_gather(d, arrival=True).wait_recv()
+
+    def drain(self):
+        self.core_copy().wait_send()
+        for d in range(1, NX):
+            self.x_copy(d).wait_send()
+            self.x_gather(d).wait_send()
+        for d in range(1, NY):
+            self.y_copy(d).wait_send()
+            self.y_gather(d).wait_send()
+        for d in range(1, NZ):
+            self.z_copy(d).wait_send()
+        for d in range(NX):
+            self.core_gather(d).wait_send()
+
+    def block(self, index):
+        per = PART // 128
+        core, rest = divmod(index, NX * per)
+        x, place = divmod(rest, per)
+        return self.full[core, x, place * 128 : (place + 1) * 128]
+
+    def unpack(self, wgrad, ggrad, bgrad):
+        for tap in range(10):
+            pair, odd = divmod(tap, 2)
+            low = slice(64 * odd, 64 * odd + 64)
+            target = ggrad if tap == 9 else wgrad.at[tap]
+            dtype = F32 if tap == 9 else BF16
+            target[0:128, 0:128] = self.block(tap).astype(dtype)
+            target[0:128, 128:192] = self.block(15 + pair)[:, low].astype(dtype)
+            target[128:192, 0:128] = self.block(10 + pair)[low].astype(dtype)
+            half, side = divmod(10 + pair, 2)
+            corner = self.block(15 + half)[low, 64 * side : 64 * side + 64]
+            target[128:192, 128:192] = corner.astype(dtype)
+        offsets = self.block(23).astype(F32)
+        bgrad[0:1, 0:128] = offsets[0:1]
+        bgrad[0:1, 128:192] = offsets[1:2, 0:64]
+
+
+def reduction_scratch():
+    return [
+        pltpu.VMEM((2, NX, PART, 128), BF16),
+        pltpu.VMEM((2, NX, PART, 128), BF16),
+        pltpu.VMEM((2, NX - 1, PART, 128), BF16),
+        pltpu.VMEM((2, NX - 1, PART, 128), BF16),
+        pltpu.VMEM((2, NY - 1, SHARD, 128), BF16),
+        pltpu.VMEM((2, NY - 1, SHARD, 128), BF16),
+        pltpu.VMEM((2, NZ, SHARD, 128), BF16),
+        pltpu.VMEM((2, NY, SHARD, 128), BF16),
+        pltpu.VMEM((2, 2, NX, PART, 128), BF16),
+        pltpu.VMEM((2, NY, SHARD, 128), F32),
+        pltpu.SemaphoreType.DMA((2, SLOTS)),
+        pltpu.SemaphoreType.DMA((2, SLOTS)),
+    ]
+
+
+def reductions(grads, scratch):
+    *buffers, send, recv = scratch
+    return [
+        Reduction(layer, grads.at[layer], *[buffer.at[layer] for buffer in buffers], send, recv)
+        for layer in range(2)
+    ]
+
+
+def reduce_kernel(grads, w1, g1, b1, w2, g2, b2, *scratch):
+    barrier = pltpu.get_barrier_semaphore()
+    met = partners()
+    for device in met:
+        pl.semaphore_signal(barrier, inc=1, device_id=device, device_id_type=MESH)
+    pl.semaphore_wait(barrier, len(met))
+    one, two = reductions(grads, scratch)
+    two.start_core()
+    one.start_core()
+    two.core_to_x()
+    one.core_to_x()
+    two.x_to_y()
+    one.x_to_y()
+    two.y_to_z()
+    one.y_to_z()
+    two.z_to_y()
+    one.z_to_y()
+    two.y_to_x()
+    one.y_to_x()
+    two.x_to_core()
+    one.x_to_core()
+    two.core_done()
+    two.unpack(w2, g2, b2)
+    one.core_done()
+    one.unpack(w1, g1, b1)
+    two.drain()
+    one.drain()
+
+
+def pack(wgrad, ggrad, bgrad):
+    turned = jnp.concatenate([wgrad.reshape(9, 192, 192), ggrad[None]]).transpose(0, 2, 1)
+    right = turned[:, :, 128:].reshape(5, 2, 192, 64).transpose(0, 2, 1, 3).reshape(5, 192, 128)
+    tiles = jnp.concatenate([turned[:, :, :128], right])
+    lower = jnp.concatenate([tiles[:, 128:].reshape(960, 128), jnp.zeros((64, 128), F32)]).reshape(8, 128, 128)
+    offsets = jnp.pad(bgrad, (0, 64)).reshape(2, 128).T
+    last = jnp.pad(offsets, ((0, 0), (0, 126)))[None]
+    blocks = jnp.concatenate([tiles[:, :128], lower, last])
+    return blocks.reshape(2, NX, PART, 128)
+
+
+def reduce_all(packed):
+    shapes = [
+        jax.ShapeDtypeStruct((9, 192, 192), BF16),
+        jax.ShapeDtypeStruct((192, 192), F32),
+        jax.ShapeDtypeStruct((1, 192), F32),
+    ] * 2
+    outs = pl.pallas_call(
+        reduce_kernel,
+        out_shape=shapes,
+        in_specs=[pl.BlockSpec(memory_space=pltpu.VMEM)],
+        out_specs=[pl.BlockSpec(memory_space=pltpu.VMEM)] * 6,
+        scratch_shapes=reduction_scratch(),
+        compiler_params=pltpu.CompilerParams(
+            collective_id=0, has_side_effects=True, vmem_limit_bytes=48 * 1024 * 1024
+        ),
+    )(packed)
+    return outs
 def padded_2(block, sides, width, periodic):
     for axis, dim in sides:
         count = lax.axis_size(axis)
@@ -129,11 +414,6 @@
     )
     beta_grad = -0.5 * jnp.sum(flat, axis=0)
     return (lower, gamma_grad, beta_grad)
-
-
-def combine_grads(wgrad, ggrad, bgrad):
-    wsum, gsum, bsum = lax.psum((wgrad, ggrad, bgrad), ("lat", "lon"))
-    return (wsum.astype(jnp.bfloat16), gsum, bsum)
 
 
 def per_device(
@@ -159,13 +439,14 @@
     )
     grad_two = dz_two.astype(jnp.bfloat16)
     wgrad_two = weight_grad(padded_h, grad_two)
-    wgrad_two, ggrad_two, bgrad_two = combine_grads(wgrad_two, ggrad_two, bgrad_two)
     dhidden = unborder(spread(grad_two, second_weight))
     dz_one, ggrad_one, bgrad_one = denormalize(dhidden, z_first, scale_one, sq_one, first_gamma)
     grad_one = dz_one.astype(jnp.bfloat16)
     wgrad_one = weight_grad(padded_x, grad_one)
-    wgrad_one, ggrad_one, bgrad_one = combine_grads(wgrad_one, ggrad_one, bgrad_one)
-    return (encoded, wgrad_one, ggrad_one, bgrad_one, wgrad_two, ggrad_two, bgrad_two)
+    packed = jnp.stack([pack(wgrad_one, ggrad_one, bgrad_one), pack(wgrad_two, ggrad_two, bgrad_two)])
+    w1, g1, b1, w2, g2, b2 = reduce_all(packed)
+    shape = (3, 3, 192, 192)
+    return (encoded, w1.reshape(shape), g1, b1.reshape(192), w2.reshape(shape), g2, b2.reshape(192))
 
 
 def solution(mesh):

time: 401 us -> 183 us (0.46)
  waiting for transfers between devices: 162 us -> 7.65 us
  blocking collectives: 126 us -> 0 us
  Pallas kernels: 0 us -> 58.2 us
  between operations: 15 us -> 1.75 us
  other arithmetic: 1.75 us -> 12.8 us
  local copies, waits for them, and re-layouts: 12 us -> 17.9 us
    psum x1 -> x0, waiting for transfers between devices: 153 us -> none  [combine_grads(): wsum, gsum, bsum = lax.psum((wgrad, ggrad, bgrad), ('lat', 'lon'))]
    psum x1 -> x0, blocking collectives: 126 us -> none  [combine_grads(): wsum, gsum, bsum = lax.psum((wgrad, ggrad, bgrad), ('lat', 'lon'))]
    pallas_call x0 -> x1, Pallas kernels: none -> 58.2 us  [reduce_all(): pl.pallas_call(reduce_kernel, out_shape=shapes, in_specs=[pl.BlockSpec(me...]
  transfers between devices with their start and end apart: 16 -> 15, of which waited for: 6 -> 6; matrix products, arithmetic and copies ran while one was open for 1% -> 5% of each run, Pallas kernels for 0% -> 0%
where the time goes in v1:
time: 183 us; the launch traced here: 182 us
  starting transfers between devices  65.5 us (36%)
  Pallas kernels  58.2 us (32%)
  matrix products  18.2 us (10%)
  local copies, waits for them, and re-layouts  17.9 us (10%)
  other arithmetic  12.8 us (7%)
  waiting for transfers between devices  7.65 us (4%)
    pallas_call x1, Pallas kernels, reduce_all(): pl.pallas_call(reduce_kernel, out_shape=shapes, in_specs=[pl.BlockSpec(me...  58.2 us
    ppermute x6, starting transfers between devices, padded_2(): lax.ppermute(lax.slice_in_dim(block, 0, width, axis=dim), axis, backward)  26.1 us
    ppermute x6, starting transfers between devices, padded_2(): lax.ppermute(lax.slice_in_dim(block, block.shape[dim] - width, None, axis...  19.8 us
    ppermute x3, starting transfers between devices, from_behind(): return lax.ppermute(block, axis, route)  19.6 us
    unnamed x49, local copies, waits for them, and re-layouts  6.35 us
    dot_general x18, matrix products, convolve(): jnp.dot(window, weight[row_off, col_off], preferred_element_type=jnp.floa...  4.52 us
    dot_general x2, matrix products, normalize(): lax.dot_general(sq.reshape(-1, chans), gamma, (((1,), (1,)), ((), ())), p...  4.5 us
    dot_general x18, matrix products, weight_grad(): lax.dot_general(window, flat, (((0,), (0,)), ((), ())), preferred_element...  4.46 us
  transfers between devices with their start and end apart: 15, of which 6 were waited for; matrix products, arithmetic and copies ran while one was open for 5% of the time, Pallas kernels for 0%

profile of v1, /device:TPU:1, one launch (start us, length us, event | category | flops | bytes accessed | tf_op | source)
XLA Modules:
  0.0 181.9 jit_solution(11661223926249588550)
XLA Ops:
  1.4 11.5 %collective-permute-start = (bf16[2,16,192]{2,1,0:T(8,128)(2,1)S(1)}, bf16[2,16,192]{2,1,0:T(8,128)(2,1)S(1)}, u32[]{:S(2)}, u32[]{:S(2)}) collective-permute-start(bf16[2,16,192]{2,1,0:T(8,128)(2,1)S(1)} %pad_maximum_fusion.21), channel_id=1, source_target_pairs={{16,0},{17,1},{18,2},{19,3},{20,4},{21,5},{22,6},{23,7},{24,8},{25... | collective-permute-start | bytes 36872 | tf_op jit(solution)/shard_map/ppermute | solution.py:310
  12.9 3.1 %collective-permute-start.1 = (bf16[1,16,192]{2,1,0:T(8,128)(2,1)S(1)}, bf16[1,16,192]{2,1,0:T(8,128)(2,1)S(1)}, u32[]{:S(2)}, u32[]{:S(2)}) collective-permute-start(bf16[1,16,192]{2,1,0:T(8,128)(2,1)S(1)} %get-tuple-element.101), channel_id=1, source_target_pairs={{0,32},{32,64},{64,96},{96,128},{128,160},{160,192},{192,224},{224... | collective-permute-start | bytes 18440 | tf_op jit(solution)/shard_map/ppermute | solution.py:299
  16.0 1.3 collective-permute-start.2
  18.3 2.1 %collective-permute-done.2 = bf16[1,16,192]{2,1,0:T(8,128)(2,1)S(1)} collective-permute-done((bf16[1,16,192]{2,1,0:T(8,128)(2,1)S(1)}, bf16[1,16,192]{2,1,0:T(8,128)(2,1)S(1)}, u32[]{:S(2)}, u32[]{:S(2)}) %collective-permute-start.2) | collective-permute-done | bytes 6176 | tf_op jit(solution)/shard_map/ppermute | solution.py:302
  20.5 4.3 %collective-permute-start.4 = (bf16[26,1,192]{2,0,1:T(8,128)(2,1)S(1)}, bf16[26,1,192]{2,0,1:T(8,128)(2,1)S(1)}, u32[]{:S(2)}, u32[]{:S(2)}) collective-permute-start(bf16[26,1,192]{2,0,1:T(8,128)(2,1)S(1)} %get-tuple-element.89), channel_id=1, source_target_pairs={{1,0},{2,1},{3,2},{4,3},{5,4},{6,5},{7,6},{8,7},{9,8},{10,9},{11,1... | collective-permute-start | bytes 29960 | tf_op jit(solution)/shard_map/ppermute | solution.py:302
  24.8 3.0 %collective-permute-start.3 = (bf16[26,1,192]{2,0,1:T(8,128)(2,1)S(1)}, bf16[26,1,192]{2,0,1:T(8,128)(2,1)S(1)}, u32[]{:S(2)}, u32[]{:S(2)}) collective-permute-start(bf16[26,1,192]{2,0,1:T(8,128)(2,1)S(1)} %get-tuple-element.90), channel_id=1, source_target_pairs={{0,1},{1,2},{2,3},{3,4},{4,5},{5,6},{6,7},{7,8},{8,9},{9,10},{10,1... | collective-permute-start | bytes 29960 | tf_op jit(solution)/shard_map/ppermute | solution.py:299
  33.0 2.2 %multiply_convert_fusion.1 = (bf16[24,16,192]{2,1,0:T(8,128)(2,1)S(1)}, f32[24,16,192]{2,1,0:T(8,128)}) fusion(f32[24,16,192]{2,1,0:T(8,128)S(1)} %bitcast.332, f32[24,16,192]{2,1,0:T(8,128)S(1)} %bitcast.354, f32[192,192]{1,0:T(8,128)} %param.18, f32[192]{0:T(256)S(1)} %copy-done.20), kind=kOutput, calls=%fused_computation.88 | convolution fusion | flops 170090496 | bytes 1180416 | tf_op jit(solution)/shard_map/dot_general | solution.py:399
  35.2 6.2 %collective-permute-start.5 = (bf16[2,16,192]{2,1,0:T(8,128)(2,1)S(1)}, bf16[2,16,192]{2,1,0:T(8,128)(2,1)S(1)}, u32[]{:S(2)}, u32[]{:S(2)}) collective-permute-start(bf16[2,16,192]{2,1,0:T(8,128)(2,1)S(1)} %pad_maximum_fusion.22), channel_id=1, source_target_pairs={{16,0},{17,1},{18,2},{19,3},{20,4},{21,5},{22,6},{23,7},{24,8},{25... | collective-permute-start | bytes 36872 | tf_op jit(solution)/shard_map/ppermute | solution.py:310
  41.4 1.3 collective-permute-start.7
  42.7 4.7 %collective-permute-start.6 = (bf16[1,16,192]{2,1,0:T(8,128)(2,1)S(1)}, bf16[1,16,192]{2,1,0:T(8,128)(2,1)S(1)}, u32[]{:S(2)}, u32[]{:S(2)}) collective-permute-start(bf16[1,16,192]{2,1,0:T(8,128)(2,1)S(1)} %get-tuple-element.98), channel_id=1, source_target_pairs={{0,32},{32,64},{64,96},{96,128},{128,160},{160,192},{192,224},{224... | collective-permute-start | bytes 18440 | tf_op jit(solution)/shard_map/ppermute | solution.py:299
  48.4 9.7 %collective-permute-start.9 = (bf16[26,1,192]{2,1,0:T(2,128)(2,1)S(1)}, bf16[26,1,192]{2,1,0:T(2,128)(2,1)S(1)}, u32[]{:S(2)}, u32[]{:S(2)}) collective-permute-start(bf16[26,1,192]{2,1,0:T(2,128)(2,1)S(1)} %get-tuple-element.93), channel_id=1, source_target_pairs={{1,0},{2,1},{3,2},{4,3},{5,4},{6,5},{7,6},{8,7},{9,8},{10,9},{11,1... | collective-permute-start | bytes 29960 | tf_op jit(solution)/shard_map/ppermute | solution.py:302
  58.1 1.9 %collective-permute-start.8 = (bf16[26,1,192]{2,1,0:T(2,128)(2,1)S(1)}, bf16[26,1,192]{2,1,0:T(2,128)(2,1)S(1)}, u32[]{:S(2)}, u32[]{:S(2)}) collective-permute-start(bf16[26,1,192]{2,1,0:T(2,128)(2,1)S(1)} %get-tuple-element.94), channel_id=1, source_target_pairs={{0,1},{1,2},{2,3},{3,4},{4,5},{5,6},{6,7},{7,8},{8,9},{9,10},{10,1... | collective-permute-start | bytes 29960 | tf_op jit(solution)/shard_map/ppermute | solution.py:299
  64.7 2.3 %fusion.44 = (f32[192]{0:T(256)S(1)}, bf16[24,16,192]{2,1,0:T(8,128)(2,1)}, f32[24,16,192]{2,1,0:T(8,128)S(1)}) fusion(f32[24,16,192]{2,1,0:T(8,128)S(1)} %bitcast.341, bf16[24,16,192]{2,1,0:T(8,128)(2,1)} %param.23, f32[24,16,192]{2,1,0:T(8,128)} %bitcast.353, f32[192,192]{1,0:T(8,128)S(1)} %copy-done, f32[192]{0:T(256)S(1)} %copy-done.19), kind=kOutput, calls=%fused_computation.107 | convolution fusion | flops 170532672 | bytes 1328640 | tf_op jit(solution)/shard_map/dot_general | solution.py:399
  74.3 8.2 %collective-permute-start.11 = (bf16[26,1,192]{2,1,0:T(2,128)(2,1)}, bf16[26,1,192]{2,1,0:T(2,128)(2,1)}, u32[]{:S(2)}, u32[]{:S(2)}) collective-permute-start(bf16[26,1,192]{2,1,0:T(2,128)(2,1)} %get-tuple-element.74), channel_id=1, source_target_pairs={{1,0},{2,1},{3,2},{4,3},{5,4},{6,5},{7,6},{8,7},{9,8},{10,9},{11,1... | collective-permute-start | bytes 29960 | tf_op jit(solution)/shard_map/ppermute | solution.py:302
  82.5 1.9 %collective-permute-start.10 = (bf16[26,1,192]{2,1,0:T(2,128)(2,1)S(1)}, bf16[26,1,192]{2,1,0:T(2,128)(2,1)}, u32[]{:S(2)}, u32[]{:S(2)}) collective-permute-start(bf16[26,1,192]{2,1,0:T(2,128)(2,1)S(1)} %get-tuple-element.73), channel_id=1, source_target_pairs={{0,1},{1,2},{2,3},{3,4},{4,5},{5,6},{6,7},{7,8},{8,9},{9,10},{10,1... | collective-permute-start | bytes 29960 | tf_op jit(solution)/shard_map/ppermute | solution.py:299
  89.5 5.1 %collective-permute-start.13 = (f32[1,16,192]{2,1,0:T(8,128)}, f32[1,16,192]{2,1,0:T(8,128)}, u32[]{:S(2)}, u32[]{:S(2)}) collective-permute-start(f32[1,16,192]{2,1,0:T(8,128)} %get-tuple-element.72), channel_id=1, source_target_pairs={{0,32},{32,64},{64,96},{96,128},{128,160},{160,192},{192,224},{224... | collective-permute-start | bytes 36872 | tf_op jit(solution)/shard_map/ppermute | solution.py:299
  94.7 1.3 pad_maximum_fusion.11
  96.0 1.9 %collective-permute-start.12 = (f32[2,16,192]{2,1,0:T(8,128)}, f32[2,16,192]{2,1,0:T(8,128)}, u32[]{:S(2)}, u32[]{:S(2)}) collective-permute-start(f32[2,16,192]{2,1,0:T(8,128)} %pad_maximum_fusion.11), channel_id=1, source_target_pairs={{16,0},{17,1},{18,2},{19,3},{20,4},{21,5},{22,6},{23,7},{24,8},{25... | collective-permute-start | bytes 73736 | tf_op jit(solution)/shard_map/ppermute | solution.py:310
  100.8 1.3 collective-permute-start.14
  102.1 2.9 %collective-permute-done.12 = f32[2,16,192]{2,1,0:T(8,128)} collective-permute-done((f32[2,16,192]{2,1,0:T(8,128)}, f32[2,16,192]{2,1,0:T(8,128)}, u32[]{:S(2)}, u32[]{:S(2)}) %collective-permute-start.12) | collective-permute-done | bytes 24608 | tf_op jit(solution)/shard_map/ppermute | solution.py:310
  114.6 1.5 pad_maximum_fusion.1
  116.1 1.6 copy.101
  117.8 1.6 pad_maximum_fusion.grads
  119.4 58.2 %shard_map.135 = (bf16[9,192,192]{2,1,0:T(8,128)(2,1)S(1)}, f32[192,192]{1,0:T(8,128)S(1)}, f32[1,192]{1,0:T(1,128)S(1)}, bf16[9,192,192]{2,1,0:T(8,128)(2,1)S(1...) custom-call(f32[2,2,4,384,128]{4,3,2,1,0:T(8,128)S(1)} %pad_maximum_fusion.grads), custom_call_target="tpu_custom_call" | custom-call | tf_op jit(solution)/shard_map/pallas_call | solution.py:281
  (174 shorter events, 40.9 us)
Async XLA Ops:
  0.6 64.1 %copy-start = (f32[192,192]{1,0:T(8,128)S(1)}, f32[192,192]{1,0:T(8,128)}, u32[]{:S(2)}) copy-start(f32[192,192]{1,0:T(8,128)} %param.21) | copy-start | bytes 442372
  1.4 19.0 %collective-permute-start = (bf16[2,16,192]{2,1,0:T(8,128)(2,1)S(1)}, bf16[2,16,192]{2,1,0:T(8,128)(2,1)S(1)}, u32[]{:S(2)}, u32[]{:S(2)}) collective-permute-start(bf16[2,16,192]{2,1,0:T(8,128)(2,1)S(1)} %pad_maximum_fusion.21), channel_id=1, source_target_pairs={{16,0},{17,1},{18,2},{19,3},{20,4},{21,5},{22,6},{23,7},{24,8},{25... | collective-permute-start | bytes 36872 | tf_op jit(solution)/shard_map/ppermute | solution.py:310
  12.9 5.4 %collective-permute-start.1 = (bf16[1,16,192]{2,1,0:T(8,128)(2,1)S(1)}, bf16[1,16,192]{2,1,0:T(8,128)(2,1)S(1)}, u32[]{:S(2)}, u32[]{:S(2)}) collective-permute-start(bf16[1,16,192]{2,1,0:T(8,128)(2,1)S(1)} %get-tuple-element.101), channel_id=1, source_target_pairs={{0,32},{32,64},{64,96},{96,128},{128,160},{160,192},{192,224},{224... | collective-permute-start | bytes 18440 | tf_op jit(solution)/shard_map/ppermute | solution.py:299
  16.0 4.4 %collective-permute-start.2 = (bf16[1,16,192]{2,1,0:T(8,128)(2,1)S(1)}, bf16[1,16,192]{2,1,0:T(8,128)(2,1)S(1)}, u32[]{:S(2)}, u32[]{:S(2)}) collective-permute-start(bf16[1,16,192]{2,1,0:T(8,128)(2,1)S(1)} %get-tuple-element.102), channel_id=1, source_target_pairs={{32,0},{64,32},{96,64},{128,96},{160,128},{192,160},{224,192},{256... | collective-permute-start | bytes 18440 | tf_op jit(solution)/shard_map/ppermute | solution.py:302
  20.5 7.6 %collective-permute-start.4 = (bf16[26,1,192]{2,0,1:T(8,128)(2,1)S(1)}, bf16[26,1,192]{2,0,1:T(8,128)(2,1)S(1)}, u32[]{:S(2)}, u32[]{:S(2)}) collective-permute-start(bf16[26,1,192]{2,0,1:T(8,128)(2,1)S(1)} %get-tuple-element.89), channel_id=1, source_target_pairs={{1,0},{2,1},{3,2},{4,3},{5,4},{6,5},{7,6},{8,7},{9,8},{10,9},{11,1... | collective-permute-start | bytes 29960 | tf_op jit(solution)/shard_map/ppermute | solution.py:302
  24.8 3.9 %collective-permute-start.3 = (bf16[26,1,192]{2,0,1:T(8,128)(2,1)S(1)}, bf16[26,1,192]{2,0,1:T(8,128)(2,1)S(1)}, u32[]{:S(2)}, u32[]{:S(2)}) collective-permute-start(bf16[26,1,192]{2,0,1:T(8,128)(2,1)S(1)} %get-tuple-element.90), channel_id=1, source_target_pairs={{0,1},{1,2},{2,3},{3,4},{4,5},{5,6},{6,7},{7,8},{8,9},{9,10},{10,1... | collective-permute-start | bytes 29960 | tf_op jit(solution)/shard_map/ppermute | solution.py:299
  32.6 27.4 %copy-start.4 = (bf16[3,3,192,192]{3,2,1,0:T(8,128)(2,1)S(1)}, bf16[3,3,192,192]{3,2,1,0:T(8,128)(2,1)}, u32[]{:S(2)}) copy-start(bf16[3,3,192,192]{3,2,1,0:T(8,128)(2,1)} %param.20) | copy-start | bytes 1990660
  32.8 28.6 %copy-start.1 = (f32[384,192]{1,0:T(8,128)}, f32[384,192]{1,0:T(8,128)S(1)}, u32[]{:S(2)}) copy-start(f32[384,192]{1,0:T(8,128)S(1)} %copy.82) | copy-start | bytes 884740
  35.2 13.0 %collective-permute-start.5 = (bf16[2,16,192]{2,1,0:T(8,128)(2,1)S(1)}, bf16[2,16,192]{2,1,0:T(8,128)(2,1)S(1)}, u32[]{:S(2)}, u32[]{:S(2)}) collective-permute-start(bf16[2,16,192]{2,1,0:T(8,128)(2,1)S(1)} %pad_maximum_fusion.22), channel_id=1, source_target_pairs={{16,0},{17,1},{18,2},{19,3},{20,4},{21,5},{22,6},{23,7},{24,8},{25... | collective-permute-start | bytes 36872 | tf_op jit(solution)/shard_map/ppermute | solution.py:310
  41.4 6.0 %collective-permute-start.7 = (bf16[1,16,192]{2,1,0:T(8,128)(2,1)S(1)}, bf16[1,16,192]{2,1,0:T(8,128)(2,1)S(1)}, u32[]{:S(2)}, u32[]{:S(2)}) collective-permute-start(bf16[1,16,192]{2,1,0:T(8,128)(2,1)S(1)} %get-tuple-element.97), channel_id=1, source_target_pairs={{32,0},{64,32},{96,64},{128,96},{160,128},{192,160},{224,192},{256... | collective-permute-start | bytes 18440 | tf_op jit(solution)/shard_map/ppermute | solution.py:302
  42.7 5.5 %collective-permute-start.6 = (bf16[1,16,192]{2,1,0:T(8,128)(2,1)S(1)}, bf16[1,16,192]{2,1,0:T(8,128)(2,1)S(1)}, u32[]{:S(2)}, u32[]{:S(2)}) collective-permute-start(bf16[1,16,192]{2,1,0:T(8,128)(2,1)S(1)} %get-tuple-element.98), channel_id=1, source_target_pairs={{0,32},{32,64},{64,96},{96,128},{128,160},{160,192},{192,224},{224... | collective-permute-start | bytes 18440 | tf_op jit(solution)/shard_map/ppermute | solution.py:299
  48.4 11.9 %collective-permute-start.9 = (bf16[26,1,192]{2,1,0:T(2,128)(2,1)S(1)}, bf16[26,1,192]{2,1,0:T(2,128)(2,1)S(1)}, u32[]{:S(2)}, u32[]{:S(2)}) collective-permute-start(bf16[26,1,192]{2,1,0:T(2,128)(2,1)S(1)} %get-tuple-element.93), channel_id=1, source_target_pairs={{1,0},{2,1},{3,2},{4,3},{5,4},{6,5},{7,6},{8,7},{9,8},{10,9},{11,1... | collective-permute-start | bytes 29960 | tf_op jit(solution)/shard_map/ppermute | solution.py:302
  58.1 3.1 %collective-permute-start.8 = (bf16[26,1,192]{2,1,0:T(2,128)(2,1)S(1)}, bf16[26,1,192]{2,1,0:T(2,128)(2,1)S(1)}, u32[]{:S(2)}, u32[]{:S(2)}) collective-permute-start(bf16[26,1,192]{2,1,0:T(2,128)(2,1)S(1)} %get-tuple-element.94), channel_id=1, source_target_pairs={{0,1},{1,2},{2,3},{3,4},{4,5},{5,6},{6,7},{7,8},{8,9},{9,10},{10,1... | collective-permute-start | bytes 29960 | tf_op jit(solution)/shard_map/ppermute | solution.py:299
  74.3 12.2 %collective-permute-start.11 = (bf16[26,1,192]{2,1,0:T(2,128)(2,1)}, bf16[26,1,192]{2,1,0:T(2,128)(2,1)}, u32[]{:S(2)}, u32[]{:S(2)}) collective-permute-start(bf16[26,1,192]{2,1,0:T(2,128)(2,1)} %get-tuple-element.74), channel_id=1, source_target_pairs={{1,0},{2,1},{3,2},{4,3},{5,4},{6,5},{7,6},{8,7},{9,8},{10,9},{11,1... | collective-permute-start | bytes 29960 | tf_op jit(solution)/shard_map/ppermute | solution.py:302
  82.5 4.0 %collective-permute-start.10 = (bf16[26,1,192]{2,1,0:T(2,128)(2,1)S(1)}, bf16[26,1,192]{2,1,0:T(2,128)(2,1)}, u32[]{:S(2)}, u32[]{:S(2)}) collective-permute-start(bf16[26,1,192]{2,1,0:T(2,128)(2,1)S(1)} %get-tuple-element.73), channel_id=1, source_target_pairs={{0,1},{1,2},{2,3},{3,4},{4,5},{5,6},{6,7},{7,8},{8,9},{9,10},{10,1... | collective-permute-start | bytes 29960 | tf_op jit(solution)/shard_map/ppermute | solution.py:299
  85.4 12.5 %copy-start.18 = (f32[1,128,128]{1,2,0:T(8,128)S(1)}, f32[1,128,128]{1,2,0:T(8,128)}, u32[]{:S(2)}) copy-start(f32[1,128,128]{1,2,0:T(8,128)} %pad_bitcast_fusion) | copy-start | bytes 196612
  88.9 9.1 %copy-start.9 = (f32[26,16,192]{2,1,0:T(8,128)}, f32[26,16,192]{2,1,0:T(8,128)S(1)}, u32[]{:S(2)}) copy-start(f32[26,16,192]{2,1,0:T(8,128)S(1)} %scatter-add.15) | copy-start | bytes 958468
  89.5 12.5 %collective-permute-start.13 = (f32[1,16,192]{2,1,0:T(8,128)}, f32[1,16,192]{2,1,0:T(8,128)}, u32[]{:S(2)}, u32[]{:S(2)}) collective-permute-start(f32[1,16,192]{2,1,0:T(8,128)} %get-tuple-element.72), channel_id=1, source_target_pairs={{0,32},{32,64},{64,96},{96,128},{128,160},{160,192},{192,224},{224... | collective-permute-start | bytes 36872 | tf_op jit(solution)/shard_map/ppermute | solution.py:299
  96.0 9.0 %collective-permute-start.12 = (f32[2,16,192]{2,1,0:T(8,128)}, f32[2,16,192]{2,1,0:T(8,128)}, u32[]{:S(2)}, u32[]{:S(2)}) collective-permute-start(f32[2,16,192]{2,1,0:T(8,128)} %pad_maximum_fusion.11), channel_id=1, source_target_pairs={{16,0},{17,1},{18,2},{19,3},{20,4},{21,5},{22,6},{23,7},{24,8},{25... | collective-permute-start | bytes 73736 | tf_op jit(solution)/shard_map/ppermute | solution.py:310
  99.6 8.5 %copy-start.2 = (f32[384,192]{1,0:T(8,128)S(1)}, f32[384,192]{1,0:T(8,128)}, u32[]{:S(2)}) copy-start(f32[384,192]{1,0:T(8,128)} %copy-done.1) | copy-start | bytes 884740
  99.6 8.5 %copy-start.3 = (f32[24,16,192]{2,1,0:T(8,128)S(1)}, f32[24,16,192]{2,1,0:T(8,128)}, u32[]{:S(2)}) copy-start(f32[24,16,192]{2,1,0:T(8,128)} %get-tuple-element.110) | copy-start | bytes 884740
  99.6 8.5 %copy-start.16 = (f32[192,192]{1,0:T(8,128)S(1)}, f32[192,192]{1,0:T(8,128)}, u32[]{:S(2)}) copy-start(f32[192,192]{1,0:T(8,128)} %param.18) | copy-start | bytes 442372
  99.6 9.0 %copy-start.8 = (bf16[26,17,192]{2,0,1:T(8,128)(2,1)S(1)}, bf16[26,17,192]{2,0,1:T(8,128)(2,1)}, u32[]{:S(2)}) copy-start(bf16[26,17,192]{2,0,1:T(8,128)(2,1)} %copy-done.7) | copy-start | bytes 509188
  100.8 5.4 %collective-permute-start.14 = (f32[1,16,192]{2,1,0:T(8,128)S(1)}, f32[1,16,192]{2,1,0:T(8,128)S(1)}, u32[]{:S(2)}, u32[]{:S(2)}) collective-permute-start(f32[1,16,192]{2,1,0:T(8,128)S(1)} %get-tuple-element.71), channel_id=1, source_target_pairs={{32,0},{64,32},{96,64},{128,96},{160,128},{192,160},{224,192},{256... | collective-permute-start | bytes 36872 | tf_op jit(solution)/shard_map/ppermute | solution.py:302
  (12 other events, 16.8 us)

commit v2 on v1

--- a/solution.py
+++ b/solution.py
@@ -1,5 +1,3 @@
-import functools
-
 import jax
 import jax.numpy as jnp
 from jax import lax
@@ -232,188 +230,260 @@
     ]
 
 
-def reduce_kernel(grads, w1, g1, b1, w2, g2, b2, *scratch):
+def neighbours():
+    lat, lon = lax.axis_index("lat"), lax.axis_index("lon")
+    lats, lons = lax.axis_size("lat"), lax.axis_size("lon")
+    first = (lat == 0).astype(jnp.int32)
+    last = (lat == lats - 1).astype(jnp.int32)
+    rows = []
+    for pole, step, side in ((first, -1, 1), (last, 1, 0)):
+        for east in (-1, 0, 1):
+            device = (lat + step * (1 - pole), lax.rem(lon + lons + east + pole * (lons // 2), lons))
+            landing = side + pole * (1 - 2 * side)
+            rows.append((device, landing * 3 + 1 - east))
+    west = (lat, lax.rem(lon + lons - 1, lons))
+    east = (lat, lax.rem(lon + 1, lons))
+    return first, last, rows, west, east
+
+
+def dot(left, right, dims=((1,), (0,))):
+    return lax.dot_general(left, right, (dims, ((), ())), preferred_element_type=F32)
+
+
+def split(value):
+    high = value.astype(BF16)
+    return high, (value - high.astype(F32)).astype(BF16)
+
+
+def dot_split(left, right, dims=((1,), (0,))):
+    left_high, left_low = split(left)
+    right_high, right_low = split(right)
+    return dot(left_high, right_high, dims) + dot(left_high, right_low, dims) + dot(left_low, right_high, dims)
+
+
+def flat(value):
+    return value.reshape(-1, value.shape[-1])
+
+
+def keep_shifted(store, value):
+    store[0] = pltpu.roll(value, 1, axis=1)
+    store[1] = value
+    store[2] = pltpu.roll(value, 23, axis=1)
+
+
+def outer_window(store, rows, ghosts, a, b, first, last):
+    turned = 2 - 2 * a
+    top = store[b, pl.ds(a + first * turned, ghosts)]
+    middle = store[b, ghosts + a : rows - ghosts + a]
+    bottom = store[b, pl.ds(rows - ghosts + a + last * turned, ghosts)]
+    return flat(jnp.concatenate([top, middle, bottom], axis=0)).astype(BF16)
+
+
+def inner_window(store, a, b, start):
+    return flat(store[b, start + a : start + a + 24, 0:16]).astype(BF16)
+
+
+def outer_convolution(store, weight, rows, ghosts, first, last):
+    total = None
+    for a in range(3):
+        for b in range(3):
+            term = dot(outer_window(store, rows, ghosts, a, b, first, last), weight[3 * a + b])
+            total = term if total is None else total + term
+    return total
+
+
+def place_block(grads, index, value):
+    per = PART // 128
+    core, rest = divmod(index, NX * per)
+    x, place = divmod(rest, per)
+    grads[core, x, place * 128 : (place + 1) * 128] = value
+
+
+def place_lower(grads, tile, value):
+    per = PART // 128
+    core, rest = divmod(15 + tile // 2, NX * per)
+    x, place = divmod(rest, per)
+    start = place * 128 + 64 * (tile % 2)
+    grads[core, x, start : start + 64] = value
+
+
+def pack_gradients(grads, store, start, grad, lever, sq, turn):
+    turned = grad.T.astype(BF16)
+    kept = None
+    for tap in range(10):
+        if tap < 9:
+            block = dot(turned, inner_window(store, tap // 3, tap % 3, start))
+        else:
+            block = -0.5 * dot_split(sq.T, lever)
+        place_block(grads, tap, block[0:128, 0:128])
+        place_lower(grads, tap, block[128:192, 0:128])
+        if tap % 2 == 0:
+            kept = block[:, 128:192]
+        else:
+            both = jnp.concatenate([kept, block[:, 128:192]], axis=1)
+            tile = 10 + tap // 2
+            place_block(grads, tile, both[0:128])
+            place_lower(grads, tile, both[128:192])
+    offsets = -0.5 * jnp.sum(lever, axis=0, keepdims=True)
+    turn[...] = jnp.zeros_like(turn)
+    turn[0:1, :] = offsets[:, 0:128]
+    turn[1:2, 0:64] = offsets[:, 128:192]
+    place_lower(grads, 15, jnp.zeros((64, 128), F32))
+    place_block(grads, 23, turn[...].T)
+
+
+def kernel(
+    x, w1, gamma1, beta1, w2, gamma2, beta2, cot,
+    encoded, out_w1, out_g1, out_b1, out_w2, out_g2, out_b2,
+    grads, top_out, bottom_out, west_out, east_out, rows_in, west_in, east_in, halo_send, halo_recv,
+    field, cotangent, x_store, h_store, g_store, z_keep, scale_keep, turn, stage, strips, *scratch,
+):
     barrier = pltpu.get_barrier_semaphore()
-    met = partners()
+    first, last, rows, west, east = neighbours()
+    met = partners() + [device for device, _ in rows] + [west, east]
     for device in met:
         pl.semaphore_signal(barrier, inc=1, device_id=device, device_id_type=MESH)
+
+    field[3:27, 0:16] = x[...].astype(F32)
+    cotangent[1:25, 0:16] = cot[...].astype(F32)
+    top_out[0] = cot[0]
+    bottom_out[0] = cot[23]
+    for k in range(3):
+        top_out[1 + k] = x[k]
+        bottom_out[1 + k] = x[23 - k]
+
+    def strip(target, tile, places, edge):
+        for half, lanes in enumerate((128, 64)):
+            span = slice(128 * half, 128 * half + lanes)
+            for ref, chosen, at_row in ((x, places, 0), (cot, (edge,), 72)):
+                stage.reshape(24, 8, 128)[:, :, 0:lanes] = ref[:, tile : tile + 8, span].astype(F32)
+                for k, place in enumerate(chosen):
+                    rows24 = stage[pl.ds(place - tile, 24, stride=8), :]
+                    strips[half, at_row + 24 * k : at_row + 24 * k + 24] = rows24
+        target[...] = strips[...].astype(BF16)
+
+    strip(west_out, 0, (0, 1, 2), 0)
+    strip(east_out, 8, (13, 14, 15), 15)
+
     pl.semaphore_wait(barrier, len(met))
+
+    def halo(source, target, sent, landed, device):
+        return pltpu.make_async_remote_copy(
+            src_ref=source,
+            dst_ref=target,
+            send_sem=halo_send.at[sent],
+            recv_sem=halo_recv.at[landed],
+            device_id=device,
+            device_id_type=MESH,
+        )
+
+    copies = [halo(west_out, east_in, 6, 6, west), halo(east_out, west_in, 7, 7, east)]
+    for index, (device, slot) in enumerate(rows):
+        source = top_out if index < 3 else bottom_out
+        copies.append(halo(source, rows_in.at[slot], index, slot, device))
+    for copy in copies:
+        copy.start()
+
+    for slot in range(6):
+        halo(top_out, rows_in.at[slot], 0, slot, rows[0][0]).wait_recv()
+    lane8 = lax.broadcasted_iota(jnp.int32, (8, 192), 0)
+    for side in range(2):
+        for k in range(4):
+            target = cotangent if k == 0 else field
+            if k == 0:
+                row = 25 * side
+            else:
+                row = 26 + k if side else 3 - k
+            target[row, 0:16] = rows_in[3 * side + 1, k].astype(F32)
+            from_west = rows_in[3 * side, k].astype(F32)[8:16]
+            from_east = rows_in[3 * side + 2, k].astype(F32)[0:8]
+            target[row, 16:24] = jnp.where(lane8 < 4, from_east, from_west)
+    copies[0].wait_recv()
+    copies[1].wait_recv()
+    for half, lanes in enumerate((128, 64)):
+        span = slice(128 * half, 128 * half + lanes)
+        for target, start, size in ((field, 3, 3), (cotangent, 1, 1)):
+            for source, offset in ((east_in, 0), (west_in, 8 - size)):
+                arrived = source[half].astype(F32)
+                for k in range(size):
+                    at_row = 24 * k if size == 3 else 72
+                    stage[pl.ds(offset + k, 24, stride=8), :] = arrived[at_row : at_row + 24]
+            target[start : start + 24, 16:24, span] = stage.reshape(24, 8, 128)[:, :, 0:lanes]
+
+    keep_shifted(x_store, field[...])
+    z1 = outer_convolution(x_store, w1, 28, 2, first, last)
+    scale1 = lax.rsqrt(beta1[...] + dot_split(z1 * z1, gamma1[...], ((1,), (1,))))
+    hidden = (z1 * scale1).astype(BF16).astype(F32)
+    keep_shifted(h_store, hidden.reshape(28, 24, 192))
+    z_keep[...] = flat(z1.reshape(28, 24, 192)[2:26, 0:16])
+    scale_keep[...] = flat(scale1.reshape(28, 24, 192)[2:26, 0:16])
+
+    z2 = outer_convolution(h_store, w2, 26, 1, first, last)
+    sq2 = z2 * z2
+    scale2 = lax.rsqrt(beta2[...] + dot_split(sq2, gamma2[...], ((1,), (1,))))
+    encoded[...] = (z2 * scale2).reshape(26, 24, 192)[1:25, 0:16].astype(BF16)
+    upper = flat(cotangent[...])
+    lever2 = upper * z2 * scale2 * scale2 * scale2
+    lower2 = upper * scale2 - z2 * dot_split(lever2, gamma2[...])
+    grad2 = lower2.astype(BF16).astype(F32).reshape(26, 24, 192)
+    keep_shifted(g_store, grad2)
+
+    def inside(value):
+        return flat(value.reshape(26, 24, 192)[1:25, 0:16])
+
     one, two = reductions(grads, scratch)
+    pack_gradients(grads.at[1], h_store, 1, inside(grad2), inside(lever2), inside(sq2), turn)
     two.start_core()
+
+    total = None
+    blank = jnp.zeros((1, 16, 192), F32)
+    for a in range(3):
+        for b in range(3):
+            shifted = g_store.at[2 - b]
+            if a == 0:
+                window = jnp.concatenate([shifted[2:25, 0:16], blank], axis=0)
+            elif a == 1:
+                window = shifted[1:25, 0:16]
+            else:
+                window = jnp.concatenate([blank, shifted[1:24, 0:16]], axis=0)
+            term = dot(flat(window).astype(BF16), w2[3 * a + b], ((1,), (1,)))
+            total = term if total is None else total + term
+    ghosts = []
+    for row, a in ((0, 2 - 2 * first), (25, 2 * last)):
+        ghost = None
+        for b in range(3):
+            term = dot(g_store[2 - b, row, 0:16].astype(BF16), w2[3 * a + b], ((1,), (1,)))
+            ghost = term if ghost is None else ghost + term
+        ghosts.append(ghost)
+    upper1 = jnp.concatenate([total[0:16] + ghosts[0], total[16:368], total[368:384] + ghosts[1]], axis=0)
+    two.core_to_x()
+
+    z1 = z_keep[...]
+    scale1 = scale_keep[...]
+    lever1 = upper1 * z1 * scale1 * scale1 * scale1
+    lower1 = upper1 * scale1 - z1 * dot_split(lever1, gamma1[...])
+    grad1 = lower1.astype(BF16).astype(F32)
+    pack_gradients(grads.at[0], x_store, 2, grad1, lever1, z1 * z1, turn)
     one.start_core()
-    two.core_to_x()
+    two.x_to_y()
     one.core_to_x()
-    two.x_to_y()
+    two.y_to_z()
     one.x_to_y()
-    two.y_to_z()
+    two.z_to_y()
     one.y_to_z()
-    two.z_to_y()
+    two.y_to_x()
     one.z_to_y()
-    two.y_to_x()
+    two.x_to_core()
     one.y_to_x()
-    two.x_to_core()
+    two.core_done()
+    two.unpack(out_w2, out_g2, out_b2)
     one.x_to_core()
-    two.core_done()
-    two.unpack(w2, g2, b2)
     one.core_done()
-    one.unpack(w1, g1, b1)
+    one.unpack(out_w1, out_g1, out_b1)
+    for copy in copies:
+        copy.wait_send()
     two.drain()
     one.drain()
-
-
-def pack(wgrad, ggrad, bgrad):
-    turned = jnp.concatenate([wgrad.reshape(9, 192, 192), ggrad[None]]).transpose(0, 2, 1)
-    right = turned[:, :, 128:].reshape(5, 2, 192, 64).transpose(0, 2, 1, 3).reshape(5, 192, 128)
-    tiles = jnp.concatenate([turned[:, :, :128], right])
-    lower = jnp.concatenate([tiles[:, 128:].reshape(960, 128), jnp.zeros((64, 128), F32)]).reshape(8, 128, 128)
-    offsets = jnp.pad(bgrad, (0, 64)).reshape(2, 128).T
-    last = jnp.pad(offsets, ((0, 0), (0, 126)))[None]
-    blocks = jnp.concatenate([tiles[:, :128], lower, last])
-    return blocks.reshape(2, NX, PART, 128)
-
-
-def reduce_all(packed):
-    shapes = [
-        jax.ShapeDtypeStruct((9, 192, 192), BF16),
-        jax.ShapeDtypeStruct((192, 192), F32),
-        jax.ShapeDtypeStruct((1, 192), F32),
-    ] * 2
-    outs = pl.pallas_call(
-        reduce_kernel,
-        out_shape=shapes,
-        in_specs=[pl.BlockSpec(memory_space=pltpu.VMEM)],
-        out_specs=[pl.BlockSpec(memory_space=pltpu.VMEM)] * 6,
-        scratch_shapes=reduction_scratch(),
-        compiler_params=pltpu.CompilerParams(
-            collective_id=0, has_side_effects=True, vmem_limit_bytes=48 * 1024 * 1024
-        ),
-    )(packed)
-    return outs
-def padded_2(block, sides, width, periodic):
-    for axis, dim in sides:
-        count = lax.axis_size(axis)
-        forward = [(i, i + 1) for i in range(count - 1)]
-        if periodic:
-            forward.append((count - 1, 0))
-        backward = [(target, source) for source, target in forward]
-        low = lax.ppermute(
-            lax.slice_in_dim(block, block.shape[dim] - width, None, axis=dim), axis, forward
-        )
-        high = lax.ppermute(lax.slice_in_dim(block, 0, width, axis=dim), axis, backward)
-        block = jnp.concatenate([low, block, high], axis=dim)
-    return block
-
-
-def from_behind(block, axis, distance):
-    devices = range(lax.axis_size(axis))
-    route = [((i - distance) % len(devices), i) for i in devices]
-    return lax.ppermute(block, axis, route)
-
-
-def border(field):
-    half = lax.axis_size("lon") // 2
-    last_band = lax.axis_size("lat") - 1
-    band = lax.axis_index("lat")
-    rows = padded_2(field, (("lat", 0),), 1, False)
-    edges = jnp.stack([field[0], field[-1]])
-    folded = from_behind(edges, "lon", half)
-    top_row = jnp.where(band == 0, folded[0], rows[0])
-    bottom_row = jnp.where(band == last_band, folded[1], rows[-1])
-    rows = jnp.concatenate([top_row[None], rows[1:-1], bottom_row[None]], axis=0)
-    return padded_2(rows, (("lon", 1),), 1, True)
-
-
-def unborder(grad):
-    half = lax.axis_size("lon") // 2
-    last_band = lax.axis_size("lat") - 1
-    band = lax.axis_index("lat")
-    sides = jnp.stack([grad[:, 0], grad[:, -1]], axis=1)
-    arrived = padded_2(sides.astype(jnp.bfloat16), (("lon", 1),), 1, True).astype(sides.dtype)
-    rows = grad[:, 1:-1]
-    rows = rows.at[:, 0].add(arrived[:, 0]).at[:, -1].add(arrived[:, -1])
-    edges = jnp.stack([rows[0], rows[-1]])
-    returned = from_behind(edges, "lon", half)
-    across = padded_2(edges, (("lat", 0),), 1, False)
-    top_add = jnp.where(band == 0, returned[0], across[0])
-    bottom_add = jnp.where(band == last_band, returned[1], across[-1])
-    inner = rows[1:-1]
-    inner = inner.at[0].add(top_add)
-    inner = inner.at[-1].add(bottom_add)
-    return inner
-
-
-def convolve(padded, weight):
-    rows_n = padded.shape[0] - 2
-    cols_n = padded.shape[1] - 2
-    chans = padded.shape[2]
-    total = jnp.zeros((rows_n * cols_n, weight.shape[3]), jnp.float32)
-    for row_off in range(3):
-        for col_off in range(3):
-            window = padded[row_off : row_off + rows_n, col_off : col_off + cols_n].reshape(
-                -1, chans
-            )
-            total = total + jnp.dot(
-                window, weight[row_off, col_off], preferred_element_type=jnp.float32
-            )
-    return total.reshape(rows_n, cols_n, -1)
-
-
-def spread(grad, weight):
-    rows_n, cols_n, outs_n = grad.shape
-    flat = grad.reshape(-1, outs_n)
-    total = jnp.zeros((rows_n + 2, cols_n + 2, weight.shape[2]), jnp.float32)
-    for row_off in range(3):
-        for col_off in range(3):
-            term = lax.dot_general(
-                flat,
-                weight[row_off, col_off],
-                (((1,), (1,)), ((), ())),
-                preferred_element_type=jnp.float32,
-            )
-            term = term.reshape(rows_n, cols_n, -1)
-            total = total + jnp.pad(term, ((row_off, 2 - row_off), (col_off, 2 - col_off), (0, 0)))
-    return total
-
-
-def weight_grad(padded, grad):
-    rows_n, cols_n, outs_n = grad.shape
-    chans = padded.shape[2]
-    flat = grad.reshape(-1, outs_n)
-    pieces = []
-    for row_off in range(3):
-        for col_off in range(3):
-            window = padded[row_off : row_off + rows_n, col_off : col_off + cols_n].reshape(
-                -1, chans
-            )
-            pieces.append(
-                lax.dot_general(
-                    window, flat, (((0,), (0,)), ((), ())), preferred_element_type=jnp.float32
-                )
-            )
-    return jnp.stack(pieces).reshape(3, 3, chans, outs_n)
-
-
-def normalize(z, gamma, beta):
-    chans = z.shape[2]
-    sq = z * z
-    summed = lax.dot_general(
-        sq.reshape(-1, chans), gamma, (((1,), (1,)), ((), ())), precision=lax.Precision.HIGHEST
-    )
-    scale = lax.rsqrt(beta + summed.reshape(z.shape))
-    return (z * scale, scale, sq)
-
-
-def denormalize(upper, z, scale, sq, gamma):
-    chans = z.shape[2]
-    lever = upper * z * scale * scale * scale
-    flat = lever.reshape(-1, chans)
-    mixed = jnp.dot(flat, gamma, precision=lax.Precision.HIGHEST).reshape(z.shape)
-    lower = upper * scale - z * mixed
-    gamma_grad = -0.5 * lax.dot_general(
-        flat, sq.reshape(-1, chans), (((0,), (0,)), ((), ())), precision=lax.Precision.HIGHEST
-    )
-    beta_grad = -0.5 * jnp.sum(flat, axis=0)
-    return (lower, gamma_grad, beta_grad)
 
 
 def per_device(
@@ -426,26 +496,54 @@
     second_beta,
     cotangent,
 ):
-    padded_x = border(fields)
-    z_first = convolve(padded_x, first_weight)
-    h_first, scale_one, sq_one = normalize(z_first, first_gamma, first_beta)
-    hidden = h_first.astype(jnp.bfloat16)
-    padded_h = border(hidden)
-    z_second = convolve(padded_h, second_weight)
-    out_float, scale_two, sq_two = normalize(z_second, second_gamma, second_beta)
-    encoded = out_float.astype(jnp.bfloat16)
-    dz_two, ggrad_two, bgrad_two = denormalize(
-        cotangent.astype(jnp.float32), z_second, scale_two, sq_two, second_gamma
+    gradients = [
+        jax.ShapeDtypeStruct((9, 192, 192), BF16),
+        jax.ShapeDtypeStruct((192, 192), F32),
+        jax.ShapeDtypeStruct((1, 192), F32),
+    ]
+    vmem = pl.BlockSpec(memory_space=pltpu.VMEM)
+    shape = (3, 3, 192, 192)
+    encoded, w1, g1, b1, w2, g2, b2 = pl.pallas_call(
+        kernel,
+        out_shape=[jax.ShapeDtypeStruct((24, 16, 192), BF16)] + gradients * 2,
+        in_specs=[vmem] * 8,
+        out_specs=[vmem] * 7,
+        scratch_shapes=[
+            pltpu.VMEM((2, 2, NX, PART, 128), F32),
+            pltpu.VMEM((4, 16, 192), BF16),
+            pltpu.VMEM((4, 16, 192), BF16),
+            pltpu.VMEM((2, 96, 128), BF16),
+            pltpu.VMEM((2, 96, 128), BF16),
+            pltpu.VMEM((6, 4, 16, 192), BF16),
+            pltpu.VMEM((2, 96, 128), BF16),
+            pltpu.VMEM((2, 96, 128), BF16),
+            pltpu.SemaphoreType.DMA((8,)),
+            pltpu.SemaphoreType.DMA((8,)),
+            pltpu.VMEM((30, 24, 192), F32),
+            pltpu.VMEM((26, 24, 192), F32),
+            pltpu.VMEM((3, 30, 24, 192), F32),
+            pltpu.VMEM((3, 28, 24, 192), F32),
+            pltpu.VMEM((3, 26, 24, 192), F32),
+            pltpu.VMEM((384, 192), F32),
+            pltpu.VMEM((384, 192), F32),
+            pltpu.VMEM((128, 128), F32),
+            pltpu.VMEM((192, 128), F32),
+            pltpu.VMEM((2, 96, 128), F32),
+            *reduction_scratch(),
+        ],
+        compiler_params=pltpu.CompilerParams(
+            collective_id=0, has_side_effects=True, vmem_limit_bytes=48 * 1024 * 1024
+        ),
+    )(
+        fields,
+        first_weight.reshape(9, 192, 192),
+        first_gamma,
+        first_beta.reshape(1, 192),
+        second_weight.reshape(9, 192, 192),
+        second_gamma,
+        second_beta.reshape(1, 192),
+        cotangent,
     )
-    grad_two = dz_two.astype(jnp.bfloat16)
-    wgrad_two = weight_grad(padded_h, grad_two)
-    dhidden = unborder(spread(grad_two, second_weight))
-    dz_one, ggrad_one, bgrad_one = denormalize(dhidden, z_first, scale_one, sq_one, first_gamma)
-    grad_one = dz_one.astype(jnp.bfloat16)
-    wgrad_one = weight_grad(padded_x, grad_one)
-    packed = jnp.stack([pack(wgrad_one, ggrad_one, bgrad_one), pack(wgrad_two, ggrad_two, bgrad_two)])
-    w1, g1, b1, w2, g2, b2 = reduce_all(packed)
-    shape = (3, 3, 192, 192)
     return (encoded, w1.reshape(shape), g1, b1.reshape(192), w2.reshape(shape), g2, b2.reshape(192))
 
 

time: 183 us -> 85.5 us (0.47)
  starting transfers between devices: 65.5 us -> 0 us
  matrix products: 18.2 us -> 0 us
  Pallas kernels: 58.2 us -> 72.8 us
  other arithmetic: 12.8 us -> 0 us
  waiting for transfers between devices: 7.65 us -> 0 us
  local copies, waits for them, and re-layouts: 17.9 us -> 11.7 us
    ppermute x15 -> x0, starting transfers between devices: 65.5 us -> none  [the longest x6 26.1 us: padded_2(): lax.ppermute(lax.slice_in_dim(block, 0, width, axis=dim), axis, backward)]
    dot_general x51 -> x0, matrix products: 18.2 us -> none  [the longest x18 4.52 us: convolve(): jnp.dot(window, weight[row_off, col_off], preferred_element_type=jnp.floa...]
    pallas_call x1, Pallas kernels: 58.2 us -> 72.8 us  [per_device(): pl.pallas_call(kernel, out_shape=[jax.ShapeDtypeStruct((24, 16, 192), BF1...]
    ppermute x15 -> x0, waiting for transfers between devices: 7.65 us -> none  [the longest x3 2.92 us: from_behind(): return lax.ppermute(block, axis, route)]
    unnamed x49 -> x23, local copies, waits for them, and re-layouts: 6.35 us -> 11.7 us
    slice x23 -> x0, local copies, waits for them, and re-layouts: 4.77 us -> none  [the longest x1 1.12 us: unborder(): inner = rows[1:-1]]
    concatenate x11 -> x0, other arithmetic: 4.51 us -> none  [the longest x2 2.63 us: pack(): blocks = jnp.concatenate([tiles[:, :128], lower, last])]
    another operation x5 -> x0, other arithmetic: 3.57 us -> none  [the longest x1 1.63 us: per_device(): jnp.stack([pack(wgrad_one, ggrad_one, bgrad_one), pack(wgrad_two, ggrad_t...]
  transfers between devices with their start and end apart: 15 -> 0, of which waited for: 6 -> 0; matrix products, arithmetic and copies ran while one was open for 5% -> 0% of each run, Pallas kernels for 0% -> 0%
where the time goes in v2:
time: 85.5 us; the launch traced here: 85.2 us
  Pallas kernels  72.8 us (85%)
  local copies, waits for them, and re-layouts  11.7 us (14%)
    pallas_call x1, Pallas kernels, per_device(): pl.pallas_call(kernel, out_shape=[jax.ShapeDtypeStruct((24, 16, 192), BF1...  72.8 us
    unnamed x23, local copies, waits for them, and re-layouts  11.7 us

profile of v2, /device:TPU:1, one launch (start us, length us, event | category | flops | bytes accessed | tf_op | source)
XLA Modules:
  0.0 85.2 jit_solution(211518669611655216)
XLA Ops:
  0.6 0.0 copy-start.7
  0.6 0.0 copy-start.6
  0.7 0.7 copy-done.7
  1.3 0.0 copy-done.6
  1.3 0.0 copy-start
  1.3 1.2 %copy-done = bf16[3,3,192,192]{3,2,1,0:T(8,128)(2,1)S(1)} copy-done((bf16[3,3,192,192]{3,2,1,0:T(8,128)(2,1)S(1)}, bf16[3,3,192,192]{3,2,1,0:T(8,128)(2,1)}, u32[]{:S(2)}) %copy-start) | copy-done | bytes 663576
  2.5 0.0 copy-start.1
  2.5 1.2 %copy-done.1 = bf16[3,3,192,192]{3,2,1,0:T(8,128)(2,1)S(1)} copy-done((bf16[3,3,192,192]{3,2,1,0:T(8,128)(2,1)S(1)}, bf16[3,3,192,192]{3,2,1,0:T(8,128)(2,1)}, u32[]{:S(2)}) %copy-start.1) | copy-done | bytes 663576
  3.7 0.0 copy-start.2
  3.7 0.9 %copy-done.2 = bf16[24,16,192]{2,1,0:T(8,128)(2,1)S(1)} copy-done((bf16[24,16,192]{2,1,0:T(8,128)(2,1)S(1)}, bf16[24,16,192]{2,1,0:T(8,128)(2,1)}, u32[]{:S(2)}) %copy-start.2) | copy-done | bytes 147480
  4.6 0.0 copy-start.3
  4.6 0.9 %copy-done.3 = f32[192,192]{1,0:T(8,128)S(1)} copy-done((f32[192,192]{1,0:T(8,128)S(1)}, f32[192,192]{1,0:T(8,128)}, u32[]{:S(2)}) %copy-start.3) | copy-done | bytes 147480
  5.5 0.0 copy-start.4
  5.5 0.9 %copy-done.4 = f32[192,192]{1,0:T(8,128)S(1)} copy-done((f32[192,192]{1,0:T(8,128)S(1)}, f32[192,192]{1,0:T(8,128)}, u32[]{:S(2)}) %copy-start.4) | copy-done | bytes 147480
  6.4 0.0 copy-start.5
  6.5 0.9 %copy-done.5 = bf16[24,16,192]{2,1,0:T(8,128)(2,1)S(1)} copy-done((bf16[24,16,192]{2,1,0:T(8,128)(2,1)S(1)}, bf16[24,16,192]{2,1,0:T(8,128)(2,1)}, u32[]{:S(2)}) %copy-start.5) | copy-done | bytes 147480
  7.4 72.8 %shard_map.135 = (bf16[24,16,192]{2,1,0:T(8,128)(2,1)S(1)}, bf16[9,192,192]{2,1,0:T(8,128)(2,1)S(1)}, f32[192,192]{1,0:T(8,128)S(1)}, f32[1,192]{1,0:T(1,128)S(1...) custom-call(bf16[24,16,192]{2,1,0:T(8,128)(2,1)S(1)} %copy-done.2, ...), custom_call_target="tpu_custom_call" | custom-call | tf_op jit(solution)/shard_map/pallas_call | solution.py:506
  80.2 0.7 copy.22
  80.9 0.9 %copy.23 = bf16[3,3,192,192]{3,2,1,0:T(8,128)(2,1)} copy(bf16[3,3,192,192]{3,2,1,0:T(8,128)(2,1)S(1)} %bitcast.9) | data formatting | bytes 1327104
  81.8 0.7 copy.24
  82.5 0.6 copy.25
  83.0 0.9 %copy.26 = bf16[3,3,192,192]{3,2,1,0:T(8,128)(2,1)} copy(bf16[3,3,192,192]{3,2,1,0:T(8,128)(2,1)S(1)} %bitcast.8) | data formatting | bytes 1327104
  84.0 0.7 copy.27
  84.6 0.6 copy.28
Async XLA Ops:
  0.6 0.7 copy-start.7
  0.6 0.7 copy-start.6
  1.3 1.2 %copy-start = (bf16[3,3,192,192]{3,2,1,0:T(8,128)(2,1)S(1)}, bf16[3,3,192,192]{3,2,1,0:T(8,128)(2,1)}, u32[]{:S(2)}) copy-start(bf16[3,3,192,192]{3,2,1,0:T(8,128)(2,1)} %param.9) | copy-start | bytes 1990660
  2.5 1.2 %copy-start.1 = (bf16[3,3,192,192]{3,2,1,0:T(8,128)(2,1)S(1)}, bf16[3,3,192,192]{3,2,1,0:T(8,128)(2,1)}, u32[]{:S(2)}) copy-start(bf16[3,3,192,192]{3,2,1,0:T(8,128)(2,1)} %param.12) | copy-start | bytes 1990660
  3.7 0.9 %copy-start.2 = (bf16[24,16,192]{2,1,0:T(8,128)(2,1)S(1)}, bf16[24,16,192]{2,1,0:T(8,128)(2,1)}, u32[]{:S(2)}) copy-start(bf16[24,16,192]{2,1,0:T(8,128)(2,1)} %x.1) | copy-start | bytes 442372
  4.6 0.9 %copy-start.3 = (f32[192,192]{1,0:T(8,128)S(1)}, f32[192,192]{1,0:T(8,128)}, u32[]{:S(2)}) copy-start(f32[192,192]{1,0:T(8,128)} %gamma1.1) | copy-start | bytes 442372
  5.5 0.9 %copy-start.4 = (f32[192,192]{1,0:T(8,128)S(1)}, f32[192,192]{1,0:T(8,128)}, u32[]{:S(2)}) copy-start(f32[192,192]{1,0:T(8,128)} %gamma2.1) | copy-start | bytes 442372
  6.4 0.9 %copy-start.5 = (bf16[24,16,192]{2,1,0:T(8,128)(2,1)S(1)}, bf16[24,16,192]{2,1,0:T(8,128)(2,1)}, u32[]{:S(2)}) copy-start(bf16[24,16,192]{2,1,0:T(8,128)(2,1)} %cot.1) | copy-start | bytes 442372

commit v3 on v2

--- a/solution.py
+++ b/solution.py
@@ -333,10 +333,12 @@
 
 
 def kernel(
-    x, w1, gamma1, beta1, w2, gamma2, beta2, cot,
-    encoded, out_w1, out_g1, out_b1, out_w2, out_g2, out_b2,
+    x_far, w1_far, gamma1_far, beta1_far, w2_far, gamma2_far, beta2_far, cot_far,
+    encoded_far, out_w1_far, out_g1_far, out_b1_far, out_w2_far, out_g2_far, out_b2_far,
+    encoded, out_w1, out_g1, out_b1, out_w2, out_g2, out_b2, written,
     grads, top_out, bottom_out, west_out, east_out, rows_in, west_in, east_in, halo_send, halo_recv,
-    field, cotangent, x_store, h_store, g_store, z_keep, scale_keep, turn, stage, strips, *scratch,
+    field, cotangent, x_store, h_store, g_store, z_keep, scale_keep, turn, stage, strips,
+    x, cot, w1, gamma1, beta1, w2, gamma2, beta2, fetched, *scratch,
 ):
     barrier = pltpu.get_barrier_semaphore()
     first, last, rows, west, east = neighbours()
@@ -344,6 +346,20 @@
     for device in met:
         pl.semaphore_signal(barrier, inc=1, device_id=device, device_id_type=MESH)
 
+    pairs = [
+        (x_far, x), (cot_far, cot), (w1_far, w1), (gamma1_far, gamma1),
+        (beta1_far, beta1), (w2_far, w2), (gamma2_far, gamma2), (beta2_far, beta2),
+    ]
+    fetches = [pltpu.make_async_copy(far, near, fetched.at[i]) for i, (far, near) in enumerate(pairs)]
+    for fetch in fetches:
+        fetch.start()
+    pairs = [
+        (encoded, encoded_far), (out_w2, out_w2_far), (out_g2, out_g2_far), (out_b2, out_b2_far),
+        (out_w1, out_w1_far), (out_g1, out_g1_far), (out_b1, out_b1_far),
+    ]
+    writes = [pltpu.make_async_copy(near, far, written.at[i]) for i, (near, far) in enumerate(pairs)]
+    fetches[0].wait()
+    fetches[1].wait()
     field[3:27, 0:16] = x[...].astype(F32)
     cotangent[1:25, 0:16] = cot[...].astype(F32)
     top_out[0] = cot[0]
@@ -410,6 +426,8 @@
                     stage[pl.ds(offset + k, 24, stride=8), :] = arrived[at_row : at_row + 24]
             target[start : start + 24, 16:24, span] = stage.reshape(24, 8, 128)[:, :, 0:lanes]
 
+    for fetch in fetches[2:]:
+        fetch.wait()
     keep_shifted(x_store, field[...])
     z1 = outer_convolution(x_store, w1, 28, 2, first, last)
     scale1 = lax.rsqrt(beta1[...] + dot_split(z1 * z1, gamma1[...], ((1,), (1,))))
@@ -422,6 +440,7 @@
     sq2 = z2 * z2
     scale2 = lax.rsqrt(beta2[...] + dot_split(sq2, gamma2[...], ((1,), (1,))))
     encoded[...] = (z2 * scale2).reshape(26, 24, 192)[1:25, 0:16].astype(BF16)
+    writes[0].start()
     upper = flat(cotangent[...])
     lever2 = upper * z2 * scale2 * scale2 * scale2
     lower2 = upper * scale2 - z2 * dot_split(lever2, gamma2[...])
@@ -477,13 +496,34 @@
     one.y_to_x()
     two.core_done()
     two.unpack(out_w2, out_g2, out_b2)
+    for write in writes[1:4]:
+        write.start()
     one.x_to_core()
     one.core_done()
     one.unpack(out_w1, out_g1, out_b1)
+    for write in writes[4:]:
+        write.start()
     for copy in copies:
         copy.wait_send()
     two.drain()
     one.drain()
+    for write in writes:
+        write.wait()
+
+
+def write_out(*refs):
+    sources, targets, held = refs[:7], refs[7:14], refs[14:21]
+    came, left = refs[21:]
+    order = (1, 4, 0, 2, 5, 3, 6)
+    inward = {i: pltpu.make_async_copy(sources[i], held[i], came.at[i]) for i in order}
+    outward = {i: pltpu.make_async_copy(held[i], targets[i], left.at[i]) for i in order}
+    for i in order:
+        inward[i].start()
+    for i in order:
+        inward[i].wait()
+        outward[i].start()
+    for i in order:
+        outward[i].wait()
 
 
 def per_device(
@@ -501,14 +541,16 @@
         jax.ShapeDtypeStruct((192, 192), F32),
         jax.ShapeDtypeStruct((1, 192), F32),
     ]
-    vmem = pl.BlockSpec(memory_space=pltpu.VMEM)
     shape = (3, 3, 192, 192)
-    encoded, w1, g1, b1, w2, g2, b2 = pl.pallas_call(
+    shapes = [jax.ShapeDtypeStruct((24, 16, 192), BF16)] + gradients * 2
+    results = pl.pallas_call(
         kernel,
-        out_shape=[jax.ShapeDtypeStruct((24, 16, 192), BF16)] + gradients * 2,
-        in_specs=[vmem] * 8,
-        out_specs=[vmem] * 7,
+        out_shape=shapes,
+        in_specs=[pl.BlockSpec(memory_space=pl.ANY)] * 8,
+        out_specs=[pl.BlockSpec(memory_space=pl.ANY)] * 7,
         scratch_shapes=[
+            *[pltpu.VMEM(shape.shape, shape.dtype) for shape in shapes],
+            pltpu.SemaphoreType.DMA((7,)),
             pltpu.VMEM((2, 2, NX, PART, 128), F32),
             pltpu.VMEM((4, 16, 192), BF16),
             pltpu.VMEM((4, 16, 192), BF16),
@@ -529,10 +571,19 @@
             pltpu.VMEM((128, 128), F32),
             pltpu.VMEM((192, 128), F32),
             pltpu.VMEM((2, 96, 128), F32),
+            pltpu.VMEM((24, 16, 192), BF16),
+            pltpu.VMEM((24, 16, 192), BF16),
+            pltpu.VMEM((9, 192, 192), BF16),
+            pltpu.VMEM((192, 192), F32),
+            pltpu.VMEM((1, 192), F32),
+            pltpu.VMEM((9, 192, 192), BF16),
+            pltpu.VMEM((192, 192), F32),
+            pltpu.VMEM((1, 192), F32),
+            pltpu.SemaphoreType.DMA((8,)),
             *reduction_scratch(),
         ],
         compiler_params=pltpu.CompilerParams(
-            collective_id=0, has_side_effects=True, vmem_limit_bytes=48 * 1024 * 1024
+            collective_id=0, has_side_effects=True, vmem_limit_bytes=56 * 1024 * 1024
         ),
     )(
         fields,
@@ -544,6 +595,18 @@
         second_beta.reshape(1, 192),
         cotangent,
     )
+    encoded, w1, g1, b1, w2, g2, b2 = pl.pallas_call(
+        write_out,
+        out_shape=shapes,
+        in_specs=[pl.BlockSpec(memory_space=pl.ANY)] * 7,
+        out_specs=[pl.BlockSpec(memory_space=pl.ANY)] * 7,
+        scratch_shapes=[
+            *[pltpu.VMEM(shape.shape, shape.dtype) for shape in shapes],
+            pltpu.SemaphoreType.DMA((7,)),
+            pltpu.SemaphoreType.DMA((7,)),
+        ],
+        compiler_params=pltpu.CompilerParams(vmem_limit_bytes=56 * 1024 * 1024),
+    )(*results)
     return (encoded, w1.reshape(shape), g1, b1.reshape(192), w2.reshape(shape), g2, b2.reshape(192))
 
 

time: 85.5 us -> 77.3 us (0.904)
  local copies, waits for them, and re-layouts: 11.7 us -> 0 us
  Pallas kernels: 72.8 us -> 76.4 us
    unnamed x23 -> x0, local copies, waits for them, and re-layouts: 11.7 us -> none
    pallas_call x1 -> x2, Pallas kernels: 72.8 us -> 76.4 us  [the longest x1 73.8 us: per_device(): pl.pallas_call(kernel, out_shape=shapes, in_specs=[pl.BlockSpec(memory_sp...]
where the time goes in v3:
time: 77.3 us; the launch traced here: 77.1 us
  Pallas kernels  76.4 us (99%)
    pallas_call x1, Pallas kernels, per_device(): pl.pallas_call(kernel, out_shape=shapes, in_specs=[pl.BlockSpec(memory_sp...  73.8 us
    pallas_call x1, Pallas kernels, per_device(): pl.pallas_call(write_out, out_shape=shapes, in_specs=[pl.BlockSpec(memory...  2.68 us

profile of v3, /device:TPU:1, one launch (start us, length us, event | category | flops | bytes accessed | tf_op | source)
XLA Modules:
  0.0 77.1 jit_solution(18004908871262210650)
XLA Ops:
  0.6 73.8 %shard_map.135 = (bf16[24,16,192]{2,1,0:T(8,128)(2,1)}, bf16[9,192,192]{2,1,0:T(8,128)(2,1)}, f32[192,192]{1,0:T(8,128)}, f32[1,192]{1,0:T(1,128)}, bf16[9,192,1...) custom-call(bf16[24,16,192]{2,1,0:T(8,128)(2,1)} %x_far.1, bf16[9,192,192]{2,1,0:T(8,128)(2,1)} %bitcast.8, ...), custom_call_target="tpu_custom_call" | custom-call | tf_op jit(solution)/shard_map/pallas_call | solution.py:546
  74.4 2.7 %shard_map.136 = (bf16[24,16,192]{2,1,0:T(8,128)(2,1)}, bf16[9,192,192]{2,1,0:T(8,128)(2,1)}, f32[192,192]{1,0:T(8,128)}, f32[1,192]{1,0:T(1,128)}, bf16[9,192,1...) custom-call(bf16[24,16,192]{2,1,0:T(8,128)(2,1)} %get-tuple-element.21.refs_0_, ...), custom_call_target="tpu_custom_call" | custom-call | tf_op jit(solution)/shard_map/pallas_call | solution.py:598

commit v4 on v2

--- a/solution.py
+++ b/solution.py
@@ -9,11 +9,9 @@
 BF16 = jnp.bfloat16
 F32 = jnp.float32
 NX, NY, NZ = 4, 8, 8
-ROWS = 3072
-HALF = ROWS // 2
-PART = HALF // NX
-SHARD = PART // NY
-SLOTS = 32
+SIZES = {"x": NX, "y": NY, "z": NZ}
+CHUNKS, CHUNK, PIECE = 6, 256, 32
+SLOTS = 24
 
 
 def coordinates():
@@ -38,155 +36,213 @@
     return found
 
 
+class Link:
+    def __init__(self, axis, send, recv):
+        place = dict(zip(("core", "x", "y", "z"), coordinates()))
+        self.size, self.me = SIZES[axis], place[axis]
+        self.axis, self.place = axis, place
+        self.send_sem, self.recv_sem = send, recv
+
+    def copy(self, source, target, d):
+        place = dict(self.place)
+        place[self.axis] = lax.rem(self.me + d, self.size)
+        return pltpu.make_async_remote_copy(
+            src_ref=source,
+            dst_ref=target,
+            send_sem=self.send_sem,
+            recv_sem=self.recv_sem,
+            device_id=at(**place),
+            device_id_type=MESH,
+        )
+
+
+class Scatter(Link):
+    def __init__(self, axis, send, recv, out, into):
+        super().__init__(axis, send, recv)
+        self.out, self.into = out, into
+
+    def start(self, piece):
+        for d in range(1, self.size):
+            self.out[d - 1] = piece(lax.rem(self.me + d, self.size)).astype(BF16)
+            self.copy(self.out.at[d - 1], self.into.at[d - 1], d).start()
+
+    def finish(self, own):
+        self.copy(self.out, self.into, 1).wait_recv()
+        total = own
+        for d in range(1, self.size):
+            total = total + self.into[d - 1].astype(F32)
+        return total
+
+    def drain(self):
+        self.copy(self.out, self.into, 1).wait_send()
+
+
+class Share(Link):
+    def __init__(self, axis, send, recv, held):
+        super().__init__(axis, send, recv)
+        self.held = held
+
+    def start(self, value):
+        self.held[self.me] = value.astype(BF16)
+        for d in range(1, self.size):
+            self.copy(self.held.at[self.me], self.held.at[self.me], d).start()
+
+    def others(self):
+        span = self.held.at[0 : self.size - 1]
+        return self.copy(span, span, 1)
+
+    def finish(self):
+        self.others().wait_recv()
+
+    def total(self):
+        self.finish()
+        total = self.held[0].astype(F32)
+        for k in range(1, self.size):
+            total = total + self.held[k].astype(F32)
+        return total
+
+    def drain(self):
+        self.others().wait_send()
+
+
 class Reduction:
-    def __init__(self, layer, grads, core_out, core_in, x_out, x_in, y_out, y_in, z_in, y_all, full, sums, send, recv):
-        self.layer = layer
+    def __init__(self, layer, grads, core_out, core_in, x_out, x_in, y_out, y_in, z_out, z_in, held8, held4, sums, full, send, recv):
         self.grads, self.full = grads, full
         self.core_out, self.core_in = core_out, core_in
-        self.x_out, self.x_in = x_out, x_in
-        self.y_out, self.y_in = y_out, y_in
-        self.z_in, self.y_all = z_in, y_all
         self.sums = sums
-        self.send, self.recv = send, recv
         self.me = coordinates()
-
-    def copy(self, source, target, slot, device):
-        made = pltpu.make_async_remote_copy(
+        self.send, self.recv = send.at[layer], recv.at[layer]
+
+        def scatter(axis, slot, out, into):
+            return Scatter(axis, self.send.at[slot], self.recv.at[slot], out, into)
+
+        def share(axis, slot, held):
+            return Share(axis, self.send.at[slot], self.recv.at[slot], held)
+
+        self.a = [
+            scatter("x", 3, x_out, x_in),
+            scatter("y", 4, y_out.at[0], y_in.at[0]),
+            share("z", 5, held8.at[0]),
+            share("y", 6, held8.at[1]),
+        ]
+        self.b = [
+            scatter("y", 10, y_out.at[1], y_in.at[1]),
+            share("z", 11, held8.at[2]),
+            share("x", 12, held4.at[0]),
+            share("y", 13, held8.at[3]),
+        ]
+        self.c = [
+            scatter("z", 14, z_out, z_in),
+            share("y", 15, held8.at[4]),
+            share("x", 16, held4.at[1]),
+            share("z", 17, held8.at[5]),
+        ]
+
+    def partner_copy(self, slot, source, target):
+        core, x, y, z = self.me
+        return pltpu.make_async_remote_copy(
             src_ref=source,
             dst_ref=target,
-            send_sem=self.send.at[self.layer, slot],
-            recv_sem=self.recv.at[self.layer, slot],
-            device_id=device,
+            send_sem=self.send.at[slot],
+            recv_sem=self.recv.at[slot],
+            device_id=at(1 - core, x, y, z),
             device_id_type=MESH,
         )
-        return made
-
-    def core_copy(self):
-        core, x, y, z = self.me
-        return self.copy(self.core_out, self.core_in, 0, at(1 - core, x, y, z))
-
-    def x_copy(self, d):
-        core, x, y, z = self.me
-        return self.copy(self.x_out.at[d - 1], self.x_in.at[d - 1], d, at(core, lax.rem(x + d, NX), y, z))
-
-    def y_copy(self, d):
-        core, x, y, z = self.me
-        return self.copy(self.y_out.at[d - 1], self.y_in.at[d - 1], 3 + d, at(core, x, lax.rem(y + d, NY), z))
-
-    def z_copy(self, d):
-        core, x, y, z = self.me
-        return self.copy(self.z_in.at[z], self.z_in.at[z], 10 + d, at(core, x, y, lax.rem(z + d, NZ)))
-
-    def z_arrival(self, d):
-        core, x, y, z = self.me
-        other = lax.rem(z + NZ - d, NZ)
-        return self.copy(self.z_in.at[other], self.z_in.at[other], 10 + d, at(core, x, y, other))
-
-    def y_gather(self, d, arrival=False):
-        core, x, y, z = self.me
-        row = lax.rem(y + NY - d, NY) if arrival else y
-        ref = self.y_all.at[row]
-        return self.copy(ref, ref, 17 + d, at(core, x, lax.rem(y + d, NY), z))
-
-    def part(self, core, x):
-        return self.full.at[core, x]
+
+    def core_copies(self):
+        spans = (slice(0, 4), slice(4, 5), slice(5, 6))
+        return [self.partner_copy(i, self.core_out.at[s], self.core_in.at[s]) for i, s in enumerate(spans)]
 
     def x_gather(self, d, arrival=False):
         core, x, y, z = self.me
-        ref = self.part(core, lax.rem(x + NX - d, NX) if arrival else x)
-        return self.copy(ref, ref, 24 + d, at(core, lax.rem(x + d, NX), y, z))
+        ref = self.full.at[core, lax.rem(x + NX - d, NX) if arrival else x]
+        return Link("x", self.send.at[6 + d], self.recv.at[6 + d]).copy(ref, ref, d)
 
     def core_gather(self, d, arrival=False):
         core, x, y, z = self.me
-        ref = self.part(1 - core if arrival else core, lax.rem(x + NX - d, NX))
-        return self.copy(ref, ref, 28 + d, at(1 - core, x, y, z))
-
-    def start_core(self):
+        chunk = lax.rem(x + NX - d, NX) if d < NX else d
+        ref = self.full.at[1 - core if arrival else core, chunk]
+        return self.partner_copy(18 + d, ref, ref)
+
+    def half(self, chunk):
+        return self.grads[self.me[0], chunk] + self.core_in[chunk].astype(F32)
+
+    def start(self):
+        core = self.me[0]
+        copies = self.core_copies()
+        self.core_out[0:4] = self.grads[1 - core, 0:4].astype(BF16)
+        copies[0].start()
+        self.core_out[4:6] = self.grads[1 - core, 4:6].astype(BF16)
+        copies[1].start()
+        copies[2].start()
+
+    def step1(self):
+        copies = self.core_copies()
+        copies[0].wait_recv()
+        self.a[0].start(self.half)
+        for i, stream in ((1, self.b), (2, self.c)):
+            copies[i].wait_recv()
+            self.sums[i] = self.half(3 + i).reshape(8, PIECE, 128)
+            stream[0].start(lambda k, i=i: self.sums[i, k])
+
+    def step2(self):
         core, x, y, z = self.me
-        self.core_out[...] = self.grads[1 - core].astype(BF16)
-        self.core_copy().start()
-
-    def core_to_x(self):
+        self.sums[0] = self.a[0].finish(self.half(x)).reshape(8, PIECE, 128)
+        self.a[1].start(lambda k: self.sums[0, k])
+        self.b[1].start(self.b[0].finish(self.sums[1, y]))
+        self.c[1].start(self.c[0].finish(self.sums[2, z]))
+
+    def step3(self):
         core, x, y, z = self.me
-        self.core_copy().wait_recv()
-        for d in range(1, NX):
-            other = lax.rem(x + d, NX)
-            self.x_out[d - 1] = (self.grads[core, other] + self.core_in[other].astype(F32)).astype(BF16)
-            self.x_copy(d).start()
-        own = self.grads[core, x] + self.core_in[x].astype(F32)
-        self.sums[...] = own.reshape(self.sums.shape)
-
-    def x_to_y(self):
-        core, x, y, z = self.me
-        total = self.sums[...]
-        for d in range(1, NX):
-            self.x_copy(d).wait_recv()
-            total = total + self.x_in[d - 1].astype(F32).reshape(total.shape)
-        self.sums[...] = total
-        for d in range(1, NY):
-            self.y_out[d - 1] = self.sums[lax.rem(y + d, NY)].astype(BF16)
-            self.y_copy(d).start()
-
-    def y_to_z(self):
-        core, x, y, z = self.me
-        total = self.sums[y]
-        for d in range(1, NY):
-            self.y_copy(d).wait_recv()
-            total = total + self.y_in[d - 1].astype(F32)
-        self.z_in[z] = total.astype(BF16)
-        for d in range(1, NZ):
-            self.z_copy(d).start()
-
-    def z_to_y(self):
-        core, x, y, z = self.me
-        for d in range(1, NZ):
-            self.z_arrival(d).wait_recv()
-        total = self.z_in[0].astype(F32)
-        for place in range(1, NZ):
-            total = total + self.z_in[place].astype(F32)
-        self.y_all[y] = total.astype(BF16)
-        for d in range(1, NY):
-            self.y_gather(d).start()
-
-    def y_to_x(self):
-        core, x, y, z = self.me
-        for d in range(1, NY):
-            self.y_gather(d, arrival=True).wait_recv()
-        whole = self.y_all[...].astype(F32).reshape(PART, 128)
-        for block in range(PART // 128):
-            turned = whole[block * 128 : (block + 1) * 128].T
-            self.full[core, x, block * 128 : (block + 1) * 128] = turned.astype(BF16)
+        self.a[2].start(self.a[1].finish(self.sums[0, y]))
+        self.b[2].start(self.b[1].total())
+        self.c[2].start(self.c[1].total())
+
+    def step4(self):
+        self.a[3].start(self.a[2].total())
+        self.b[3].start(self.b[2].total())
+        self.c[3].start(self.c[2].total())
+
+    def turn(self, share, chunk):
+        share.finish()
+        whole = share.held[...].astype(F32).reshape(CHUNK, 128)
+        for block in range(2):
+            rows = slice(block * 128, block * 128 + 128)
+            self.full[self.me[0], chunk, rows] = whole[rows].T.astype(BF16)
+
+    def step5(self):
+        self.turn(self.a[3], self.me[1])
         for d in range(1, NX):
             self.x_gather(d).start()
         self.core_gather(0).start()
-
-    def x_to_core(self):
+        self.turn(self.b[3], 4)
+        self.core_gather(4).start()
+        self.turn(self.c[3], 5)
+        self.core_gather(5).start()
+
+    def step6(self):
         for d in range(1, NX):
             self.x_gather(d, arrival=True).wait_recv()
             self.core_gather(d).start()
 
-    def core_done(self):
-        for d in range(NX):
+    def step7(self):
+        for d in range(CHUNKS):
             self.core_gather(d, arrival=True).wait_recv()
 
     def drain(self):
-        self.core_copy().wait_send()
+        for copy in self.core_copies():
+            copy.wait_send()
+        for phase in self.a + self.b + self.c:
+            phase.drain()
         for d in range(1, NX):
-            self.x_copy(d).wait_send()
             self.x_gather(d).wait_send()
-        for d in range(1, NY):
-            self.y_copy(d).wait_send()
-            self.y_gather(d).wait_send()
-        for d in range(1, NZ):
-            self.z_copy(d).wait_send()
-        for d in range(NX):
+        for d in range(CHUNKS):
             self.core_gather(d).wait_send()
 
     def block(self, index):
-        per = PART // 128
-        core, rest = divmod(index, NX * per)
-        x, place = divmod(rest, per)
-        return self.full[core, x, place * 128 : (place + 1) * 128]
+        core, rest = divmod(index, 12)
+        chunk, side = divmod(rest, 2)
+        return self.full[core, chunk, side * 128 : side * 128 + 128]
 
     def unpack(self, wgrad, ggrad, bgrad):
         for tap in range(10):
@@ -207,16 +263,18 @@
 
 def reduction_scratch():
     return [
-        pltpu.VMEM((2, NX, PART, 128), BF16),
-        pltpu.VMEM((2, NX, PART, 128), BF16),
-        pltpu.VMEM((2, NX - 1, PART, 128), BF16),
-        pltpu.VMEM((2, NX - 1, PART, 128), BF16),
-        pltpu.VMEM((2, NY - 1, SHARD, 128), BF16),
-        pltpu.VMEM((2, NY - 1, SHARD, 128), BF16),
-        pltpu.VMEM((2, NZ, SHARD, 128), BF16),
-        pltpu.VMEM((2, NY, SHARD, 128), BF16),
-        pltpu.VMEM((2, 2, NX, PART, 128), BF16),
-        pltpu.VMEM((2, NY, SHARD, 128), F32),
+        pltpu.VMEM((2, CHUNKS, CHUNK, 128), BF16),
+        pltpu.VMEM((2, CHUNKS, CHUNK, 128), BF16),
+        pltpu.VMEM((2, NX - 1, CHUNK, 128), BF16),
+        pltpu.VMEM((2, NX - 1, CHUNK, 128), BF16),
+        pltpu.VMEM((2, 2, NY - 1, PIECE, 128), BF16),
+        pltpu.VMEM((2, 2, NY - 1, PIECE, 128), BF16),
+        pltpu.VMEM((2, NZ - 1, PIECE, 128), BF16),
+        pltpu.VMEM((2, NZ - 1, PIECE, 128), BF16),
+        pltpu.VMEM((2, 6, 8, PIECE, 128), BF16),
+        pltpu.VMEM((2, 2, NX, PIECE, 128), BF16),
+        pltpu.VMEM((2, 3, 8, PIECE, 128), F32),
+        pltpu.VMEM((2, 2, CHUNKS, CHUNK, 128), BF16),
         pltpu.SemaphoreType.DMA((2, SLOTS)),
         pltpu.SemaphoreType.DMA((2, SLOTS)),
     ]
@@ -293,18 +351,16 @@
 
 
 def place_block(grads, index, value):
-    per = PART // 128
-    core, rest = divmod(index, NX * per)
-    x, place = divmod(rest, per)
-    grads[core, x, place * 128 : (place + 1) * 128] = value
+    core, rest = divmod(index, 12)
+    chunk, side = divmod(rest, 2)
+    grads[core, chunk, side * 128 : side * 128 + 128] = value
 
 
 def place_lower(grads, tile, value):
-    per = PART // 128
-    core, rest = divmod(15 + tile // 2, NX * per)
-    x, place = divmod(rest, per)
-    start = place * 128 + 64 * (tile % 2)
-    grads[core, x, start : start + 64] = value
+    core, rest = divmod(15 + tile // 2, 12)
+    chunk, side = divmod(rest, 2)
+    start = side * 128 + 64 * (tile % 2)
+    grads[core, chunk, start : start + 64] = value
 
 
 def pack_gradients(grads, store, start, grad, lever, sq, turn):
@@ -333,10 +389,11 @@
 
 
 def kernel(
-    x, w1, gamma1, beta1, w2, gamma2, beta2, cot,
+    x_far, w1_far, gamma1_far, beta1_far, w2_far, gamma2_far, beta2_far, cot_far,
     encoded, out_w1, out_g1, out_b1, out_w2, out_g2, out_b2,
     grads, top_out, bottom_out, west_out, east_out, rows_in, west_in, east_in, halo_send, halo_recv,
-    field, cotangent, x_store, h_store, g_store, z_keep, scale_keep, turn, stage, strips, *scratch,
+    field, cotangent, x_store, h_store, g_store, z_keep, scale_keep, turn, stage, strips,
+    x, cot, w1, gamma1, beta1, w2, gamma2, beta2, fetched, *scratch,
 ):
     barrier = pltpu.get_barrier_semaphore()
     first, last, rows, west, east = neighbours()
@@ -344,6 +401,15 @@
     for device in met:
         pl.semaphore_signal(barrier, inc=1, device_id=device, device_id_type=MESH)
 
+    pairs = [
+        (x_far, x), (cot_far, cot), (w1_far, w1), (gamma1_far, gamma1),
+        (beta1_far, beta1), (w2_far, w2), (gamma2_far, gamma2), (beta2_far, beta2),
+    ]
+    fetches = [pltpu.make_async_copy(far, near, fetched.at[i]) for i, (far, near) in enumerate(pairs)]
+    for fetch in fetches:
+        fetch.start()
+    fetches[0].wait()
+    fetches[1].wait()
     field[3:27, 0:16] = x[...].astype(F32)
     cotangent[1:25, 0:16] = cot[...].astype(F32)
     top_out[0] = cot[0]
@@ -410,6 +476,8 @@
                     stage[pl.ds(offset + k, 24, stride=8), :] = arrived[at_row : at_row + 24]
             target[start : start + 24, 16:24, span] = stage.reshape(24, 8, 128)[:, :, 0:lanes]
 
+    for fetch in fetches[2:]:
+        fetch.wait()
     keep_shifted(x_store, field[...])
     z1 = outer_convolution(x_store, w1, 28, 2, first, last)
     scale1 = lax.rsqrt(beta1[...] + dot_split(z1 * z1, gamma1[...], ((1,), (1,))))
@@ -433,7 +501,7 @@
 
     one, two = reductions(grads, scratch)
     pack_gradients(grads.at[1], h_store, 1, inside(grad2), inside(lever2), inside(sq2), turn)
-    two.start_core()
+    two.start()
 
     total = None
     blank = jnp.zeros((1, 16, 192), F32)
@@ -456,7 +524,7 @@
             ghost = term if ghost is None else ghost + term
         ghosts.append(ghost)
     upper1 = jnp.concatenate([total[0:16] + ghosts[0], total[16:368], total[368:384] + ghosts[1]], axis=0)
-    two.core_to_x()
+    two.step1()
 
     z1 = z_keep[...]
     scale1 = scale_keep[...]
@@ -464,26 +532,35 @@
     lower1 = upper1 * scale1 - z1 * dot_split(lever1, gamma1[...])
     grad1 = lower1.astype(BF16).astype(F32)
     pack_gradients(grads.at[0], x_store, 2, grad1, lever1, z1 * z1, turn)
-    one.start_core()
-    two.x_to_y()
-    one.core_to_x()
-    two.y_to_z()
-    one.x_to_y()
-    two.z_to_y()
-    one.y_to_z()
-    two.y_to_x()
-    one.z_to_y()
-    two.x_to_core()
-    one.y_to_x()
-    two.core_done()
+    one.start()
+    two.step2()
+    one.step1()
+    two.step3()
+    one.step2()
+    two.step4()
+    one.step3()
+    two.step5()
+    one.step4()
+    two.step6()
+    one.step5()
+    two.step7()
     two.unpack(out_w2, out_g2, out_b2)
-    one.x_to_core()
-    one.core_done()
+    one.step6()
+    one.step7()
     one.unpack(out_w1, out_g1, out_b1)
     for copy in copies:
         copy.wait_send()
     two.drain()
     one.drain()
+
+
+def write_out(*refs):
+    sources, targets, done = refs[:7], refs[7:14], refs[14]
+    copies = [pltpu.make_async_copy(sources[i], targets[i], done.at[i]) for i in (1, 4, 0, 2, 5, 3, 6)]
+    for copy in copies:
+        copy.start()
+    for copy in copies:
+        copy.wait()
 
 
 def per_device(
@@ -501,15 +578,26 @@
         jax.ShapeDtypeStruct((192, 192), F32),
         jax.ShapeDtypeStruct((1, 192), F32),
     ]
-    vmem = pl.BlockSpec(memory_space=pltpu.VMEM)
     shape = (3, 3, 192, 192)
-    encoded, w1, g1, b1, w2, g2, b2 = pl.pallas_call(
+    shapes = [jax.ShapeDtypeStruct((24, 16, 192), BF16)] + gradients * 2
+    anywhere, vmem = pl.BlockSpec(memory_space=pl.ANY), pl.BlockSpec(memory_space=pltpu.VMEM)
+    operands = [
+        fields,
+        first_weight.reshape(9, 192, 192),
+        first_gamma,
+        first_beta.reshape(1, 192),
+        second_weight.reshape(9, 192, 192),
+        second_gamma,
+        second_beta.reshape(1, 192),
+        cotangent,
+    ]
+    results = pl.pallas_call(
         kernel,
-        out_shape=[jax.ShapeDtypeStruct((24, 16, 192), BF16)] + gradients * 2,
-        in_specs=[vmem] * 8,
+        out_shape=shapes,
+        in_specs=[anywhere] * 8,
         out_specs=[vmem] * 7,
         scratch_shapes=[
-            pltpu.VMEM((2, 2, NX, PART, 128), F32),
+            pltpu.VMEM((2, 2, CHUNKS, CHUNK, 128), F32),
             pltpu.VMEM((4, 16, 192), BF16),
             pltpu.VMEM((4, 16, 192), BF16),
             pltpu.VMEM((2, 96, 128), BF16),
@@ -529,21 +617,29 @@
             pltpu.VMEM((128, 128), F32),
             pltpu.VMEM((192, 128), F32),
             pltpu.VMEM((2, 96, 128), F32),
+            pltpu.VMEM((24, 16, 192), BF16),
+            pltpu.VMEM((24, 16, 192), BF16),
+            pltpu.VMEM((9, 192, 192), BF16),
+            pltpu.VMEM((192, 192), F32),
+            pltpu.VMEM((1, 192), F32),
+            pltpu.VMEM((9, 192, 192), BF16),
+            pltpu.VMEM((192, 192), F32),
+            pltpu.VMEM((1, 192), F32),
+            pltpu.SemaphoreType.DMA((8,)),
             *reduction_scratch(),
         ],
         compiler_params=pltpu.CompilerParams(
-            collective_id=0, has_side_effects=True, vmem_limit_bytes=48 * 1024 * 1024
+            collective_id=0, has_side_effects=True, vmem_limit_bytes=44 * 1024 * 1024
         ),
-    )(
-        fields,
-        first_weight.reshape(9, 192, 192),
-        first_gamma,
-        first_beta.reshape(1, 192),
-        second_weight.reshape(9, 192, 192),
-        second_gamma,
-        second_beta.reshape(1, 192),
-        cotangent,
-    )
+    )(*[pltpu.with_memory_space_constraint(operand, pltpu.HBM) for operand in operands])
+    encoded, w1, g1, b1, w2, g2, b2 = pl.pallas_call(
+        write_out,
+        out_shape=shapes,
+        in_specs=[vmem] * 7,
+        out_specs=[anywhere] * 7,
+        scratch_shapes=[pltpu.SemaphoreType.DMA((7,))],
+        compiler_params=pltpu.CompilerParams(vmem_limit_bytes=8 * 1024 * 1024),
+    )(*results)
     return (encoded, w1.reshape(shape), g1, b1.reshape(192), w2.reshape(shape), g2, b2.reshape(192))
 
 

time: 85.5 us -> 72.7 us (0.85)
  local copies, waits for them, and re-layouts: 11.7 us -> 0 us
  Pallas kernels: 72.8 us -> 71.9 us
    unnamed x23 -> x0, local copies, waits for them, and re-layouts: 11.7 us -> none
    pallas_call x1 -> x2, Pallas kernels: 72.8 us -> 71.9 us  [the longest x1 70.5 us: per_device(): pl.pallas_call(kernel, out_shape=shapes, in_specs=[anywhere] * 8, out_spe...]
where the time goes in v4:
time: 72.7 us; the launch traced here: 72.6 us
  Pallas kernels  71.9 us (99%)
    pallas_call x1, Pallas kernels, per_device(): pl.pallas_call(kernel, out_shape=shapes, in_specs=[anywhere] * 8, out_spe...  70.5 us
    pallas_call x1, Pallas kernels, per_device(): pl.pallas_call(write_out, out_shape=shapes, in_specs=[vmem] * 7, out_spec...  1.46 us

profile of v4, /device:TPU:1, one launch (start us, length us, event | category | flops | bytes accessed | tf_op | source)
XLA Modules:
  0.0 72.6 jit_solution(15059524845515377924)
XLA Ops:
  0.6 70.5 %shard_map.135 = (bf16[24,16,192]{2,1,0:T(8,128)(2,1)S(1)}, bf16[9,192,192]{2,1,0:T(8,128)(2,1)S(1)}, f32[192,192]{1,0:T(8,128)S(1)}, f32[1,192]{1,0:T(1,128)S(1...) custom-call(bf16[24,16,192]{2,1,0:T(8,128)(2,1)} %x_far.1, ...), custom_call_target="tpu_custom_call" | custom-call | tf_op jit(solution)/shard_map/pallas_call | solution.py:594
  71.1 1.5 %shard_map.136 = (bf16[24,16,192]{2,1,0:T(8,128)(2,1)}, bf16[9,192,192]{2,1,0:T(8,128)(2,1)}, f32[192,192]{1,0:T(8,128)}, f32[1,192]{1,0:T(1,128)}, bf16[9,192,1...) custom-call(bf16[24,16,192]{2,1,0:T(8,128)(2,1)S(1)} %get-tuple-element.21.refs_0_, ...), custom_call_target="tpu_custom_call" | custom-call | tf_op jit(solution)/shard_map/pallas_call | solution.py:635

commit v5 on v4

--- a/solution.py
+++ b/solution.py
@@ -10,8 +10,8 @@
 F32 = jnp.float32
 NX, NY, NZ = 4, 8, 8
 SIZES = {"x": NX, "y": NY, "z": NZ}
-CHUNKS, CHUNK, PIECE = 6, 256, 32
-SLOTS = 24
+BLOCKS = 12
+SLOTS = 36
 
 
 def coordinates():
@@ -34,6 +34,10 @@
     found += [at(core, x, lax.rem(y + d, NY), z) for d in range(1, NY)]
     found += [at(core, x, y, lax.rem(z + d, NZ)) for d in range(1, NZ)]
     return found
+
+
+def far_first(size):
+    return sorted(range(1, size), key=lambda d: -min(d, size - d))
 
 
 class Link:
@@ -62,7 +66,7 @@
         self.out, self.into = out, into
 
     def start(self, piece):
-        for d in range(1, self.size):
+        for d in far_first(self.size):
             self.out[d - 1] = piece(lax.rem(self.me + d, self.size)).astype(BF16)
             self.copy(self.out.at[d - 1], self.into.at[d - 1], d).start()
 
@@ -84,7 +88,7 @@
 
     def start(self, value):
         self.held[self.me] = value.astype(BF16)
-        for d in range(1, self.size):
+        for d in far_first(self.size):
             self.copy(self.held.at[self.me], self.held.at[self.me], d).start()
 
     def others(self):
@@ -106,143 +110,176 @@
 
 
 class Reduction:
-    def __init__(self, layer, grads, core_out, core_in, x_out, x_in, y_out, y_in, z_out, z_in, held8, held4, sums, full, send, recv):
+    def __init__(self, layer, grads, core_out, core_in, x_out, x_in, y_out, y_in, z_out, z_in, y_out2, y_in2, z_out2, z_in2, held16, held32, held4, sums16, sums32, full, send, recv):
         self.grads, self.full = grads, full
         self.core_out, self.core_in = core_out, core_in
-        self.sums = sums
         self.me = coordinates()
         self.send, self.recv = send.at[layer], recv.at[layer]
-
-        def scatter(axis, slot, out, into):
-            return Scatter(axis, self.send.at[slot], self.recv.at[slot], out, into)
-
-        def share(axis, slot, held):
-            return Share(axis, self.send.at[slot], self.recv.at[slot], held)
-
-        self.a = [
-            scatter("x", 3, x_out, x_in),
-            scatter("y", 4, y_out.at[0], y_in.at[0]),
-            share("z", 5, held8.at[0]),
-            share("y", 6, held8.at[1]),
+        self.slots = 0
+        self.streams = [
+            self.twice(0, "x", "y", "z", (x_out.at[0], x_in.at[0]), (y_out, y_in), held16.at[0], held16.at[1], sums16.at[0]),
+            self.twice(4, "x", "z", "y", (x_out.at[1], x_in.at[1]), (z_out, z_in), held16.at[2], held16.at[3], sums16.at[1]),
+            self.once(8, "y", "x", "z", (y_out2, y_in2), held4.at[0], held32.at[0], held32.at[1], sums32.at[0]),
+            self.once(10, "z", "x", "y", (z_out2, z_in2), held4.at[1], held32.at[2], held32.at[3], sums32.at[1]),
         ]
-        self.b = [
-            scatter("y", 10, y_out.at[1], y_in.at[1]),
-            share("z", 11, held8.at[2]),
-            share("x", 12, held4.at[0]),
-            share("y", 13, held8.at[3]),
-        ]
-        self.c = [
-            scatter("z", 14, z_out, z_in),
-            share("y", 15, held8.at[4]),
-            share("x", 16, held4.at[1]),
-            share("z", 17, held8.at[5]),
-        ]
-
-    def partner_copy(self, slot, source, target):
+
+    def slot(self):
+        self.slots += 1
+        return self.send.at[self.slots - 1], self.recv.at[self.slots - 1]
+
+    def place(self, axis):
+        return self.me["xyz".index(axis) + 1]
+
+    def partner_copy(self, sems, source, target):
         core, x, y, z = self.me
         return pltpu.make_async_remote_copy(
             src_ref=source,
             dst_ref=target,
-            send_sem=self.send.at[slot],
-            recv_sem=self.recv.at[slot],
+            send_sem=sems[0],
+            recv_sem=sems[1],
             device_id=at(1 - core, x, y, z),
             device_id_type=MESH,
         )
 
-    def core_copies(self):
-        spans = (slice(0, 4), slice(4, 5), slice(5, 6))
-        return [self.partner_copy(i, self.core_out.at[s], self.core_in.at[s]) for i, s in enumerate(spans)]
-
-    def x_gather(self, d, arrival=False):
-        core, x, y, z = self.me
-        ref = self.full.at[core, lax.rem(x + NX - d, NX) if arrival else x]
-        return Link("x", self.send.at[6 + d], self.recv.at[6 + d]).copy(ref, ref, d)
-
-    def core_gather(self, d, arrival=False):
-        core, x, y, z = self.me
-        chunk = lax.rem(x + NX - d, NX) if d < NX else d
-        ref = self.full.at[1 - core if arrival else core, chunk]
-        return self.partner_copy(18 + d, ref, ref)
-
-    def half(self, chunk):
-        return self.grads[self.me[0], chunk] + self.core_in[chunk].astype(F32)
-
-    def start(self):
+    def core_phase(self, first, count):
+        sems = self.slot()
+        span = slice(first, first + count)
+        copy = self.partner_copy(sems, self.core_out.at[span], self.core_in.at[span])
+
+        def start():
+            self.core_out[span] = self.grads[1 - self.me[0], span].astype(BF16)
+            copy.start()
+
+        return start, copy
+
+    def half(self, block):
+        return self.grads[self.me[0], block] + self.core_in[block].astype(F32)
+
+    def turned(self, piece):
+        return piece.astype(F32).T.astype(BF16)
+
+    def twice(self, first, axis, second, third, wide, narrow, held, spread, sums):
         core = self.me[0]
-        copies = self.core_copies()
-        self.core_out[0:4] = self.grads[1 - core, 0:4].astype(BF16)
-        copies[0].start()
-        self.core_out[4:6] = self.grads[1 - core, 4:6].astype(BF16)
-        copies[1].start()
-        copies[2].start()
-
-    def step1(self):
-        copies = self.core_copies()
-        copies[0].wait_recv()
-        self.a[0].start(self.half)
-        for i, stream in ((1, self.b), (2, self.c)):
-            copies[i].wait_recv()
-            self.sums[i] = self.half(3 + i).reshape(8, PIECE, 128)
-            stream[0].start(lambda k, i=i: self.sums[i, k])
-
-    def step2(self):
-        core, x, y, z = self.me
-        self.sums[0] = self.a[0].finish(self.half(x)).reshape(8, PIECE, 128)
-        self.a[1].start(lambda k: self.sums[0, k])
-        self.b[1].start(self.b[0].finish(self.sums[1, y]))
-        self.c[1].start(self.c[0].finish(self.sums[2, z]))
-
-    def step3(self):
-        core, x, y, z = self.me
-        self.a[2].start(self.a[1].finish(self.sums[0, y]))
-        self.b[2].start(self.b[1].total())
-        self.c[2].start(self.c[1].total())
-
-    def step4(self):
-        self.a[3].start(self.a[2].total())
-        self.b[3].start(self.b[2].total())
-        self.c[3].start(self.c[2].total())
-
-    def turn(self, share, chunk):
-        share.finish()
-        whole = share.held[...].astype(F32).reshape(CHUNK, 128)
-        for block in range(2):
-            rows = slice(block * 128, block * 128 + 128)
-            self.full[self.me[0], chunk, rows] = whole[rows].T.astype(BF16)
-
-    def step5(self):
-        self.turn(self.a[3], self.me[1])
-        for d in range(1, NX):
-            self.x_gather(d).start()
-        self.core_gather(0).start()
-        self.turn(self.b[3], 4)
-        self.core_gather(4).start()
-        self.turn(self.c[3], 5)
-        self.core_gather(5).start()
-
-    def step6(self):
-        for d in range(1, NX):
-            self.x_gather(d, arrival=True).wait_recv()
-            self.core_gather(d).start()
-
-    def step7(self):
-        for d in range(CHUNKS):
-            self.core_gather(d, arrival=True).wait_recv()
+        begin, core_copy = self.core_phase(first, 4)
+        one = Scatter(axis, *self.slot(), *wide)
+        two = Scatter(second, *self.slot(), *narrow)
+        three = Share(third, *self.slot(), held)
+        four = Share(second, *self.slot(), spread)
+        gather_sems = [self.slot() for _ in range(1, NX)]
+        last_sems = [self.slot() for _ in range(NX)]
+        me, here = self.place(axis), self.place(second)
+
+        def block(d):
+            return first + lax.rem(me + NX - d, NX)
+
+        def gather(d, arrival=False):
+            ref = self.full.at[core, block(d) if arrival else block(0)]
+            return Link(axis, *gather_sems[d - 1]).copy(ref, ref, d)
+
+        def last(d, arrival=False):
+            ref = self.full.at[1 - core if arrival else core, block(d)]
+            return self.partner_copy(last_sems[d], ref, ref)
+
+        def step1():
+            core_copy.wait_recv()
+            one.start(lambda k: self.half(first + k))
+
+        def step2():
+            sums[...] = one.finish(self.half(first + me)).reshape(sums.shape)
+            two.start(lambda k: sums[k])
+
+        def step3():
+            three.start(two.finish(sums[here]))
+
+        def step4():
+            four.start(three.total())
+
+        def step5():
+            four.finish()
+            self.full[core, block(0)] = self.turned(spread[...].reshape(128, 128))
+            for d in range(1, NX):
+                gather(d).start()
+            last(0).start()
+
+        def step6():
+            for d in range(1, NX):
+                gather(d, arrival=True).wait_recv()
+                last(d).start()
+
+        def done():
+            for d in range(NX):
+                last(d, arrival=True).wait_recv()
+
+        def drain():
+            core_copy.wait_send()
+            for phase in (one, two, three, four):
+                phase.drain()
+            for d in range(NX):
+                last(d).wait_send()
+            for d in range(1, NX):
+                gather(d).wait_send()
+
+        return (begin, step1, step2, step3, step4, step5, step6, done, drain)
+
+    def once(self, first, axis, second, third, wide, held, held_more, spread, sums):
+        core = self.me[0]
+        begin, core_copy = self.core_phase(first, 2)
+        one = Scatter(axis, *self.slot(), *wide)
+        two = Share(second, *self.slot(), held)
+        three = Share(third, *self.slot(), held_more)
+        four = Share(axis, *self.slot(), spread)
+        last_sems = self.slot()
+        me = self.place(axis)
+
+        def last(arrival=False):
+            ref = self.full.at[1 - core if arrival else core, first : first + 2]
+            return self.partner_copy(last_sems, ref, ref)
+
+        def step1():
+            core_copy.wait_recv()
+            total = self.grads[core, first : first + 2] + self.core_in[first : first + 2].astype(F32)
+            sums[...] = total.reshape(sums.shape)
+            one.start(lambda k: sums[k])
+
+        def step2():
+            two.start(one.finish(sums[me]))
+
+        def step3():
+            three.start(two.total())
+
+        def step4():
+            four.start(three.total())
+
+        def step5():
+            four.finish()
+            whole = spread[...].reshape(2, 128, 128)
+            for side in range(2):
+                self.full[core, first + side] = self.turned(whole[side])
+            last().start()
+
+        def step6():
+            pass
+
+        def done():
+            last(arrival=True).wait_recv()
+
+        def drain():
+            core_copy.wait_send()
+            for phase in (one, two, three, four):
+                phase.drain()
+            last().wait_send()
+
+        return (begin, step1, step2, step3, step4, step5, step6, done, drain)
+
+    def step(self, index, streams=(0, 1, 2, 3)):
+        for k in streams:
+            self.streams[k][index]()
 
     def drain(self):
-        for copy in self.core_copies():
-            copy.wait_send()
-        for phase in self.a + self.b + self.c:
-            phase.drain()
-        for d in range(1, NX):
-            self.x_gather(d).wait_send()
-        for d in range(CHUNKS):
-            self.core_gather(d).wait_send()
+        self.step(8)
 
     def block(self, index):
-        core, rest = divmod(index, 12)
-        chunk, side = divmod(rest, 2)
-        return self.full[core, chunk, side * 128 : side * 128 + 128]
+        return self.full[divmod(index, BLOCKS)]
 
     def unpack(self, wgrad, ggrad, bgrad):
         for tap in range(10):
@@ -263,18 +300,24 @@
 
 def reduction_scratch():
     return [
-        pltpu.VMEM((2, CHUNKS, CHUNK, 128), BF16),
-        pltpu.VMEM((2, CHUNKS, CHUNK, 128), BF16),
-        pltpu.VMEM((2, NX - 1, CHUNK, 128), BF16),
-        pltpu.VMEM((2, NX - 1, CHUNK, 128), BF16),
-        pltpu.VMEM((2, 2, NY - 1, PIECE, 128), BF16),
-        pltpu.VMEM((2, 2, NY - 1, PIECE, 128), BF16),
-        pltpu.VMEM((2, NZ - 1, PIECE, 128), BF16),
-        pltpu.VMEM((2, NZ - 1, PIECE, 128), BF16),
-        pltpu.VMEM((2, 6, 8, PIECE, 128), BF16),
-        pltpu.VMEM((2, 2, NX, PIECE, 128), BF16),
-        pltpu.VMEM((2, 3, 8, PIECE, 128), F32),
-        pltpu.VMEM((2, 2, CHUNKS, CHUNK, 128), BF16),
+        pltpu.VMEM((2, BLOCKS, 128, 128), BF16),
+        pltpu.VMEM((2, BLOCKS, 128, 128), BF16),
+        pltpu.VMEM((2, 2, NX - 1, 128, 128), BF16),
+        pltpu.VMEM((2, 2, NX - 1, 128, 128), BF16),
+        pltpu.VMEM((2, NY - 1, 16, 128), BF16),
+        pltpu.VMEM((2, NY - 1, 16, 128), BF16),
+        pltpu.VMEM((2, NZ - 1, 16, 128), BF16),
+        pltpu.VMEM((2, NZ - 1, 16, 128), BF16),
+        pltpu.VMEM((2, NY - 1, 32, 128), BF16),
+        pltpu.VMEM((2, NY - 1, 32, 128), BF16),
+        pltpu.VMEM((2, NZ - 1, 32, 128), BF16),
+        pltpu.VMEM((2, NZ - 1, 32, 128), BF16),
+        pltpu.VMEM((2, 4, 8, 16, 128), BF16),
+        pltpu.VMEM((2, 4, 8, 32, 128), BF16),
+        pltpu.VMEM((2, 2, NX, 32, 128), BF16),
+        pltpu.VMEM((2, 2, 8, 16, 128), F32),
+        pltpu.VMEM((2, 2, 8, 32, 128), F32),
+        pltpu.VMEM((2, 2, BLOCKS, 128, 128), BF16),
         pltpu.SemaphoreType.DMA((2, SLOTS)),
         pltpu.SemaphoreType.DMA((2, SLOTS)),
     ]
@@ -351,16 +394,14 @@
 
 
 def place_block(grads, index, value):
-    core, rest = divmod(index, 12)
-    chunk, side = divmod(rest, 2)
-    grads[core, chunk, side * 128 : side * 128 + 128] = value
+    core, block = divmod(index, BLOCKS)
+    grads[core, block] = value
 
 
 def place_lower(grads, tile, value):
-    core, rest = divmod(15 + tile // 2, 12)
-    chunk, side = divmod(rest, 2)
-    start = side * 128 + 64 * (tile % 2)
-    grads[core, chunk, start : start + 64] = value
+    core, block = divmod(15 + tile // 2, BLOCKS)
+    start = 64 * (tile % 2)
+    grads[core, block, start : start + 64] = value
 
 
 def pack_gradients(grads, store, start, grad, lever, sq, turn):
@@ -501,7 +542,7 @@
 
     one, two = reductions(grads, scratch)
     pack_gradients(grads.at[1], h_store, 1, inside(grad2), inside(lever2), inside(sq2), turn)
-    two.start()
+    two.step(0)
 
     total = None
     blank = jnp.zeros((1, 16, 192), F32)
@@ -524,7 +565,7 @@
             ghost = term if ghost is None else ghost + term
         ghosts.append(ghost)
     upper1 = jnp.concatenate([total[0:16] + ghosts[0], total[16:368], total[368:384] + ghosts[1]], axis=0)
-    two.step1()
+    two.step(1)
 
     z1 = z_keep[...]
     scale1 = scale_keep[...]
@@ -532,21 +573,14 @@
     lower1 = upper1 * scale1 - z1 * dot_split(lever1, gamma1[...])
     grad1 = lower1.astype(BF16).astype(F32)
     pack_gradients(grads.at[0], x_store, 2, grad1, lever1, z1 * z1, turn)
-    one.start()
-    two.step2()
-    one.step1()
-    two.step3()
-    one.step2()
-    two.step4()
-    one.step3()
-    two.step5()
-    one.step4()
-    two.step6()
-    one.step5()
-    two.step7()
+    one.step(0)
+    one.step(1)
+    two.step(2)
+    for index in range(2, 7):
+        one.step(index)
+        two.step(index + 1)
     two.unpack(out_w2, out_g2, out_b2)
-    one.step6()
-    one.step7()
+    one.step(7)
     one.unpack(out_w1, out_g1, out_b1)
     for copy in copies:
         copy.wait_send()
@@ -597,7 +631,7 @@
         in_specs=[anywhere] * 8,
         out_specs=[vmem] * 7,
         scratch_shapes=[
-            pltpu.VMEM((2, 2, CHUNKS, CHUNK, 128), F32),
+            pltpu.VMEM((2, 2, BLOCKS, 128, 128), F32),
             pltpu.VMEM((4, 16, 192), BF16),
             pltpu.VMEM((4, 16, 192), BF16),
             pltpu.VMEM((2, 96, 128), BF16),

time: 72.7 us -> 65.1 us (0.90)
  Pallas kernels: 71.9 us -> 64.3 us
    pallas_call x1, Pallas kernels: 70.5 us -> 62.9 us  [per_device(): pl.pallas_call(kernel, out_shape=shapes, in_specs=[anywhere] * 8, out_spe...]
where the time goes in v5:
time: 65.1 us; the launch traced here: 65 us
  Pallas kernels  64.3 us (99%)
    pallas_call x1, Pallas kernels, per_device(): pl.pallas_call(kernel, out_shape=shapes, in_specs=[anywhere] * 8, out_spe...  62.9 us
    pallas_call x1, Pallas kernels, per_device(): pl.pallas_call(write_out, out_shape=shapes, in_specs=[vmem] * 7, out_spec...  1.46 us

profile of v5, /device:TPU:1, one launch (start us, length us, event | category | flops | bytes accessed | tf_op | source)
XLA Modules:
  0.0 65.0 jit_solution(475516814707319952)
XLA Ops:
  0.6 62.9 %shard_map.135 = (bf16[24,16,192]{2,1,0:T(8,128)(2,1)S(1)}, bf16[9,192,192]{2,1,0:T(8,128)(2,1)S(1)}, f32[192,192]{1,0:T(8,128)S(1)}, f32[1,192]{1,0:T(1,128)S(1...) custom-call(bf16[24,16,192]{2,1,0:T(8,128)(2,1)} %x_far.1, ...), custom_call_target="tpu_custom_call" | custom-call | tf_op jit(solution)/shard_map/pallas_call | solution.py:628
  63.5 1.5 %shard_map.136 = (bf16[24,16,192]{2,1,0:T(8,128)(2,1)}, bf16[9,192,192]{2,1,0:T(8,128)(2,1)}, f32[192,192]{1,0:T(8,128)}, f32[1,192]{1,0:T(1,128)}, bf16[9,192,1...) custom-call(bf16[24,16,192]{2,1,0:T(8,128)(2,1)S(1)} %get-tuple-element.21.refs_0_, ...), custom_call_target="tpu_custom_call" | custom-call | tf_op jit(solution)/shard_map/pallas_call | solution.py:669

commit v6 on v5

--- a/solution.py
+++ b/solution.py
@@ -341,7 +341,7 @@
         for east in (-1, 0, 1):
             device = (lat + step * (1 - pole), lax.rem(lon + lons + east + pole * (lons // 2), lons))
             landing = side + pole * (1 - 2 * side)
-            rows.append((device, landing * 3 + 1 - east))
+            rows.append((device, 4 + landing if east == 0 else 2 * landing + (1 - east) // 2))
     west = (lat, lax.rem(lon + lons - 1, lons))
     east = (lat, lax.rem(lon + 1, lons))
     return first, last, rows, west, east
@@ -366,10 +366,10 @@
     return value.reshape(-1, value.shape[-1])
 
 
-def keep_shifted(store, value):
-    store[0] = pltpu.roll(value, 1, axis=1)
-    store[1] = value
-    store[2] = pltpu.roll(value, 23, axis=1)
+def keep_shifted(store, value, rows=slice(None)):
+    store[0, rows] = pltpu.roll(value, 1, axis=1)
+    store[1, rows] = value
+    store[2, rows] = pltpu.roll(value, 23, axis=1)
 
 
 def outer_window(store, rows, ghosts, a, b, first, last):
@@ -429,16 +429,19 @@
     place_block(grads, 23, turn[...].T)
 
 
-def kernel(
+def normal_scale(z, gamma, beta):
+    return lax.rsqrt(beta[...] + dot_split(z * z, gamma[...], ((1,), (1,))))
+
+
+def first_kernel(
     x_far, w1_far, gamma1_far, beta1_far, w2_far, gamma2_far, beta2_far, cot_far,
-    encoded, out_w1, out_g1, out_b1, out_w2, out_g2, out_b2,
-    grads, top_out, bottom_out, west_out, east_out, rows_in, west_in, east_in, halo_send, halo_recv,
-    field, cotangent, x_store, h_store, g_store, z_keep, scale_keep, turn, stage, strips,
-    x, cot, w1, gamma1, beta1, w2, gamma2, beta2, fetched, *scratch,
+    cotangent, x_store, h_store, z_keep, scale_keep, gamma1, w2, gamma2, beta2,
+    x, cot, w1, beta1, field, top_out, bottom_out, west_out, east_out, corner_out, middle_in, corner_in, west_in, east_in, stage, strips,
+    fetched, halo_send, halo_recv,
 ):
     barrier = pltpu.get_barrier_semaphore()
     first, last, rows, west, east = neighbours()
-    met = partners() + [device for device, _ in rows] + [west, east]
+    met = [device for device, _ in rows] + [west, east]
     for device in met:
         pl.semaphore_signal(barrier, inc=1, device_id=device, device_id_type=MESH)
 
@@ -451,13 +454,13 @@
         fetch.start()
     fetches[0].wait()
     fetches[1].wait()
-    field[3:27, 0:16] = x[...].astype(F32)
-    cotangent[1:25, 0:16] = cot[...].astype(F32)
-    top_out[0] = cot[0]
-    bottom_out[0] = cot[23]
-    for k in range(3):
-        top_out[1 + k] = x[k]
-        bottom_out[1 + k] = x[23 - k]
+    for side, out in enumerate((top_out, bottom_out)):
+        lines = [cot[23 * side]] + [x[23 - k if side else k] for k in range(3)]
+        for k, line in enumerate(lines):
+            out[k] = line
+        for edge, lanes in ((0, slice(0, 4)), (1, slice(12, 16))):
+            corner = jnp.concatenate([line.astype(F32)[lanes] for line in lines], axis=0)
+            corner_out[2 * side + edge] = corner.astype(BF16)
 
     def strip(target, tile, places, edge):
         for half, lanes in enumerate((128, 64)):
@@ -485,26 +488,21 @@
         )
 
     copies = [halo(west_out, east_in, 6, 6, west), halo(east_out, west_in, 7, 7, east)]
-    for index, (device, slot) in enumerate(rows):
-        source = top_out if index < 3 else bottom_out
-        copies.append(halo(source, rows_in.at[slot], index, slot, device))
-    for copy in copies:
+    for index in (0, 2, 3, 5, 1, 4):
+        device, slot = rows[index]
+        if index in (1, 4):
+            source, target = (top_out, bottom_out)[index // 3], middle_in.at[slot - 4]
+        else:
+            source, target = corner_out.at[2 * (index // 3) + (index % 3) // 2], corner_in.at[slot]
+        copies.append(halo(source, target, index, slot, device))
+    for copy in copies[2:] + copies[:2]:
         copy.start()
 
-    for slot in range(6):
-        halo(top_out, rows_in.at[slot], 0, slot, rows[0][0]).wait_recv()
-    lane8 = lax.broadcasted_iota(jnp.int32, (8, 192), 0)
-    for side in range(2):
-        for k in range(4):
-            target = cotangent if k == 0 else field
-            if k == 0:
-                row = 25 * side
-            else:
-                row = 26 + k if side else 3 - k
-            target[row, 0:16] = rows_in[3 * side + 1, k].astype(F32)
-            from_west = rows_in[3 * side, k].astype(F32)[8:16]
-            from_east = rows_in[3 * side + 2, k].astype(F32)[0:8]
-            target[row, 16:24] = jnp.where(lane8 < 4, from_east, from_west)
+    field[3:27, 0:16] = x[...].astype(F32)
+    cotangent[1:25, 0:16] = cot[...].astype(F32)
+    for fetch in fetches[2:]:
+        fetch.wait()
+
     copies[0].wait_recv()
     copies[1].wait_recv()
     for half, lanes in enumerate((128, 64)):
@@ -517,15 +515,65 @@
                     stage[pl.ds(offset + k, 24, stride=8), :] = arrived[at_row : at_row + 24]
             target[start : start + 24, 16:24, span] = stage.reshape(24, 8, 128)[:, :, 0:lanes]
 
-    for fetch in fetches[2:]:
-        fetch.wait()
-    keep_shifted(x_store, field[...])
-    z1 = outer_convolution(x_store, w1, 28, 2, first, last)
-    scale1 = lax.rsqrt(beta1[...] + dot_split(z1 * z1, gamma1[...], ((1,), (1,))))
-    hidden = (z1 * scale1).astype(BF16).astype(F32)
-    keep_shifted(h_store, hidden.reshape(28, 24, 192))
-    z_keep[...] = flat(z1.reshape(28, 24, 192)[2:26, 0:16])
-    scale_keep[...] = flat(scale1.reshape(28, 24, 192)[2:26, 0:16])
+    def layer(window):
+        z = None
+        for a in range(3):
+            for b in range(3):
+                term = dot(flat(window(a, b)).astype(BF16), w1[3 * a + b])
+                z = term if z is None else z + term
+        scale = normal_scale(z, gamma1, beta1)
+        hidden = (z * scale).astype(BF16).astype(F32)
+        return [value.reshape(-1, 24, 192) for value in (z, scale, hidden)]
+
+    keep_shifted(x_store, field[3:27], slice(3, 27))
+    z, scale, hidden = layer(lambda a, b: x_store[b, 3 + a : 25 + a])
+    z_keep[1:23] = z[:, 0:16]
+    scale_keep[1:23] = scale[:, 0:16]
+    keep_shifted(h_store, hidden, slice(3, 25))
+
+    for slot in range(6):
+        source, target = (top_out, middle_in.at[slot - 4]) if slot > 3 else (corner_out.at[0], corner_in.at[slot])
+        halo(source, target, 0, slot, rows[0][0]).wait_recv()
+    for side in range(2):
+        from_west = corner_in[2 * side].astype(F32)
+        from_east = corner_in[2 * side + 1].astype(F32)
+        for k in range(4):
+            target = cotangent if k == 0 else field
+            if k == 0:
+                row = 25 * side
+            else:
+                row = 26 + k if side else 3 - k
+            target[row, 0:16] = middle_in[side, k].astype(F32)
+            span = slice(4 * k, 4 * k + 4)
+            target[row, 16:24] = jnp.concatenate([from_east[span], from_west[span]], axis=0)
+    keep_shifted(x_store, field[0:3], slice(0, 3))
+    keep_shifted(x_store, field[27:30], slice(27, 30))
+
+    def edge_window(a, b):
+        top = x_store[b, pl.ds(a + first * (2 - 2 * a), 2)]
+        bottom = x_store[b, pl.ds(26 + a + last * (2 - 2 * a), 2)]
+        return jnp.concatenate([top, x_store[b, 2 + a : 3 + a], x_store[b, 25 + a : 26 + a], bottom], axis=0)
+
+    z, scale, hidden = layer(edge_window)
+    for place, row in ((0, 2), (23, 3)):
+        z_keep[place] = z[row, 0:16]
+        scale_keep[place] = scale[row, 0:16]
+    keep_shifted(h_store, hidden[0:3], slice(0, 3))
+    keep_shifted(h_store, hidden[3:6], slice(25, 28))
+    for copy in copies:
+        copy.wait_send()
+
+
+def second_kernel(
+    cotangent, x_store, h_store, z_keep, scale_keep, gamma1, w2, gamma2, beta2,
+    encoded, out_w1, out_g1, out_b1, out_w2, out_g2, out_b2,
+    grads, g_store, turn, *scratch,
+):
+    barrier = pltpu.get_barrier_semaphore()
+    first, last = neighbours()[:2]
+    met = partners()
+    for device in met:
+        pl.semaphore_signal(barrier, inc=1, device_id=device, device_id_type=MESH)
 
     z2 = outer_convolution(h_store, w2, 26, 1, first, last)
     sq2 = z2 * z2
@@ -542,6 +590,7 @@
 
     one, two = reductions(grads, scratch)
     pack_gradients(grads.at[1], h_store, 1, inside(grad2), inside(lever2), inside(sq2), turn)
+    pl.semaphore_wait(barrier, len(met))
     two.step(0)
 
     total = None
@@ -567,8 +616,8 @@
     upper1 = jnp.concatenate([total[0:16] + ghosts[0], total[16:368], total[368:384] + ghosts[1]], axis=0)
     two.step(1)
 
-    z1 = z_keep[...]
-    scale1 = scale_keep[...]
+    z1 = flat(z_keep[...])
+    scale1 = flat(scale_keep[...])
     lever1 = upper1 * z1 * scale1 * scale1 * scale1
     lower1 = upper1 * scale1 - z1 * dot_split(lever1, gamma1[...])
     grad1 = lower1.astype(BF16).astype(F32)
@@ -582,8 +631,6 @@
     two.unpack(out_w2, out_g2, out_b2)
     one.step(7)
     one.unpack(out_w1, out_g1, out_b1)
-    for copy in copies:
-        copy.wait_send()
     two.drain()
     one.drain()
 
@@ -625,47 +672,65 @@
         second_beta.reshape(1, 192),
         cotangent,
     ]
-    results = pl.pallas_call(
-        kernel,
-        out_shape=shapes,
+    carried = [
+        jax.ShapeDtypeStruct(extent, dtype)
+        for extent, dtype in (
+            ((26, 24, 192), F32),
+            ((3, 30, 24, 192), F32),
+            ((3, 28, 24, 192), F32),
+            ((24, 16, 192), F32),
+            ((24, 16, 192), F32),
+            ((192, 192), F32),
+            ((9, 192, 192), BF16),
+            ((192, 192), F32),
+            ((1, 192), F32),
+        )
+    ]
+    middle = pl.pallas_call(
+        first_kernel,
+        out_shape=carried,
         in_specs=[anywhere] * 8,
-        out_specs=[vmem] * 7,
+        out_specs=[vmem] * 9,
         scratch_shapes=[
-            pltpu.VMEM((2, 2, BLOCKS, 128, 128), F32),
+            pltpu.VMEM((24, 16, 192), BF16),
+            pltpu.VMEM((24, 16, 192), BF16),
+            pltpu.VMEM((9, 192, 192), BF16),
+            pltpu.VMEM((1, 192), F32),
+            pltpu.VMEM((30, 24, 192), F32),
             pltpu.VMEM((4, 16, 192), BF16),
             pltpu.VMEM((4, 16, 192), BF16),
             pltpu.VMEM((2, 96, 128), BF16),
             pltpu.VMEM((2, 96, 128), BF16),
-            pltpu.VMEM((6, 4, 16, 192), BF16),
+            pltpu.VMEM((4, 16, 192), BF16),
+            pltpu.VMEM((2, 4, 16, 192), BF16),
+            pltpu.VMEM((4, 16, 192), BF16),
             pltpu.VMEM((2, 96, 128), BF16),
             pltpu.VMEM((2, 96, 128), BF16),
+            pltpu.VMEM((192, 128), F32),
+            pltpu.VMEM((2, 96, 128), F32),
             pltpu.SemaphoreType.DMA((8,)),
             pltpu.SemaphoreType.DMA((8,)),
-            pltpu.VMEM((30, 24, 192), F32),
-            pltpu.VMEM((26, 24, 192), F32),
-            pltpu.VMEM((3, 30, 24, 192), F32),
-            pltpu.VMEM((3, 28, 24, 192), F32),
+            pltpu.SemaphoreType.DMA((8,)),
+        ],
+        compiler_params=pltpu.CompilerParams(
+            collective_id=0, has_side_effects=True, vmem_limit_bytes=32 * 1024 * 1024
+        ),
+    )(*[pltpu.with_memory_space_constraint(operand, pltpu.HBM) for operand in operands])
+    results = pl.pallas_call(
+        second_kernel,
+        out_shape=shapes,
+        in_specs=[vmem] * 9,
+        out_specs=[vmem] * 7,
+        scratch_shapes=[
+            pltpu.VMEM((2, 2, BLOCKS, 128, 128), F32),
             pltpu.VMEM((3, 26, 24, 192), F32),
-            pltpu.VMEM((384, 192), F32),
-            pltpu.VMEM((384, 192), F32),
             pltpu.VMEM((128, 128), F32),
-            pltpu.VMEM((192, 128), F32),
-            pltpu.VMEM((2, 96, 128), F32),
-            pltpu.VMEM((24, 16, 192), BF16),
-            pltpu.VMEM((24, 16, 192), BF16),
-            pltpu.VMEM((9, 192, 192), BF16),
-            pltpu.VMEM((192, 192), F32),
-            pltpu.VMEM((1, 192), F32),
-            pltpu.VMEM((9, 192, 192), BF16),
-            pltpu.VMEM((192, 192), F32),
-            pltpu.VMEM((1, 192), F32),
-            pltpu.SemaphoreType.DMA((8,)),
             *reduction_scratch(),
         ],
         compiler_params=pltpu.CompilerParams(
-            collective_id=0, has_side_effects=True, vmem_limit_bytes=44 * 1024 * 1024
+            collective_id=1, has_side_effects=True, vmem_limit_bytes=32 * 1024 * 1024
         ),
-    )(*[pltpu.with_memory_space_constraint(operand, pltpu.HBM) for operand in operands])
+    )(*middle)
     encoded, w1, g1, b1, w2, g2, b2 = pl.pallas_call(
         write_out,
         out_shape=shapes,

time: 65.1 us -> 61.6 us (0.946)
  Pallas kernels: 64.3 us -> 60.8 us
    pallas_call x1 -> x2, Pallas kernels: 62.9 us -> 59.3 us  [the longest x1 41.7 us: per_device(): pl.pallas_call(second_kernel, out_shape=shapes, in_specs=[vmem] * 9, out_...]
where the time goes in v6:
time: 61.6 us; the launch traced here: 61.5 us
  Pallas kernels  60.8 us (99%)
  between operations  0.65 us (1%)
    pallas_call x1, Pallas kernels, per_device(): pl.pallas_call(second_kernel, out_shape=shapes, in_specs=[vmem] * 9, out_...  41.7 us
    pallas_call x1, Pallas kernels, per_device(): pl.pallas_call(first_kernel, out_shape=carried, in_specs=[anywhere] * 8,...  17.7 us
    pallas_call x1, Pallas kernels, per_device(): pl.pallas_call(write_out, out_shape=shapes, in_specs=[vmem] * 7, out_spec...  1.46 us

profile of v6, /device:TPU:1, one launch (start us, length us, event | category | flops | bytes accessed | tf_op | source)
XLA Modules:
  0.0 61.5 jit_solution(14328646798043628470)
XLA Ops:
  0.6 17.7 %shard_map.135 = (f32[26,24,192]{2,1,0:T(8,128)S(1)}, f32[3,30,24,192]{3,2,1,0:T(8,128)S(1)}, f32[3,28,24,192]{3,2,1,0:T(8,128)S(1)}, f32[24,16,192]{2,1,0:T(8,1...) custom-call(bf16[24,16,192]{2,1,0:T(8,128)(2,1)} %x_far.1, ...), custom_call_target="tpu_custom_call" | custom-call | tf_op jit(solution)/shard_map/pallas_call | solution.py:689
  18.3 41.7 %shard_map.136 = (bf16[24,16,192]{2,1,0:T(8,128)(2,1)S(1)}, bf16[9,192,192]{2,1,0:T(8,128)(2,1)S(1)}, f32[192,192]{1,0:T(8,128)S(1)}, f32[1,192]{1,0:T(1,128)S(1...) custom-call(f32[26,24,192]{2,1,0:T(8,128)S(1)} %get-tuple-element.30.cotangent, ...), custom_call_target="tpu_custom_call" | custom-call | tf_op jit(solution)/shard_map/pallas_call | solution.py:719
  60.0 1.5 %shard_map.137 = (bf16[24,16,192]{2,1,0:T(8,128)(2,1)}, bf16[9,192,192]{2,1,0:T(8,128)(2,1)}, f32[192,192]{1,0:T(8,128)}, f32[1,192]{1,0:T(1,128)}, bf16[9,192,1...) custom-call(bf16[24,16,192]{2,1,0:T(8,128)(2,1)S(1)} %get-tuple-element.39.refs_0_, ...), custom_call_target="tpu_custom_call" | custom-call | tf_op jit(solution)/shard_map/pallas_call | solution.py:734

commit v7 on v6

--- a/solution.py
+++ b/solution.py
@@ -12,6 +12,14 @@
 SIZES = {"x": NX, "y": NY, "z": NZ}
 BLOCKS = 12
 SLOTS = 36
+DEALT = ((0, 1, 10, 15), (2, 3, 11, 16)), ((4, 5, 12, 17), (6, 7, 13, 20)), ((8, 9), (18, 21)), ((14, 19), (22, 23))
+FIRSTS = (0, 4, 8, 10)
+PLACES = {
+    part: (core, FIRSTS[stream] + k)
+    for stream, cores in enumerate(DEALT)
+    for core, parts in enumerate(cores)
+    for k, part in enumerate(parts)
+}
 
 
 def coordinates():
@@ -279,7 +287,7 @@
         self.step(8)
 
     def block(self, index):
-        return self.full[divmod(index, BLOCKS)]
+        return self.full[PLACES[index]]
 
     def unpack(self, wgrad, ggrad, bgrad):
         for tap in range(10):
@@ -394,17 +402,17 @@
 
 
 def place_block(grads, index, value):
-    core, block = divmod(index, BLOCKS)
+    core, block = PLACES[index]
     grads[core, block] = value
 
 
 def place_lower(grads, tile, value):
-    core, block = divmod(15 + tile // 2, BLOCKS)
+    core, block = PLACES[15 + tile // 2]
     start = 64 * (tile % 2)
     grads[core, block, start : start + 64] = value
 
 
-def pack_gradients(grads, store, start, grad, lever, sq, turn):
+def pack_gradients(grads, store, start, grad, lever, sq, turn, after=None):
     turned = grad.T.astype(BF16)
     kept = None
     for tap in range(10):
@@ -421,6 +429,8 @@
             tile = 10 + tap // 2
             place_block(grads, tile, both[0:128])
             place_lower(grads, tile, both[128:192])
+        if after and tap in after:
+            after[tap]()
     offsets = -0.5 * jnp.sum(lever, axis=0, keepdims=True)
     turn[...] = jnp.zeros_like(turn)
     turn[0:1, :] = offsets[:, 0:128]
@@ -430,7 +440,7 @@
 
 
 def normal_scale(z, gamma, beta):
-    return lax.rsqrt(beta[...] + dot_split(z * z, gamma[...], ((1,), (1,))))
+    return lax.rsqrt(beta[...] + dot((z * z).astype(BF16), gamma[...].astype(BF16), ((1,), (1,))))
 
 
 def first_kernel(
@@ -441,7 +451,7 @@
 ):
     barrier = pltpu.get_barrier_semaphore()
     first, last, rows, west, east = neighbours()
-    met = [device for device, _ in rows] + [west, east]
+    met = [west, east] + [device for device, _ in rows]
     for device in met:
         pl.semaphore_signal(barrier, inc=1, device_id=device, device_id_type=MESH)
 
@@ -495,7 +505,7 @@
         else:
             source, target = corner_out.at[2 * (index // 3) + (index % 3) // 2], corner_in.at[slot]
         copies.append(halo(source, target, index, slot, device))
-    for copy in copies[2:] + copies[:2]:
+    for copy in copies:
         copy.start()
 
     field[3:27, 0:16] = x[...].astype(F32)
@@ -577,11 +587,11 @@
 
     z2 = outer_convolution(h_store, w2, 26, 1, first, last)
     sq2 = z2 * z2
-    scale2 = lax.rsqrt(beta2[...] + dot_split(sq2, gamma2[...], ((1,), (1,))))
+    scale2 = normal_scale(z2, gamma2, beta2)
     encoded[...] = (z2 * scale2).reshape(26, 24, 192)[1:25, 0:16].astype(BF16)
     upper = flat(cotangent[...])
     lever2 = upper * z2 * scale2 * scale2 * scale2
-    lower2 = upper * scale2 - z2 * dot_split(lever2, gamma2[...])
+    lower2 = upper * scale2 - z2 * dot(lever2.astype(BF16), gamma2[...].astype(BF16))
     grad2 = lower2.astype(BF16).astype(F32).reshape(26, 24, 192)
     keep_shifted(g_store, grad2)
 
@@ -614,15 +624,16 @@
             ghost = term if ghost is None else ghost + term
         ghosts.append(ghost)
     upper1 = jnp.concatenate([total[0:16] + ghosts[0], total[16:368], total[368:384] + ghosts[1]], axis=0)
-    two.step(1)
 
     z1 = flat(z_keep[...])
     scale1 = flat(scale_keep[...])
     lever1 = upper1 * z1 * scale1 * scale1 * scale1
-    lower1 = upper1 * scale1 - z1 * dot_split(lever1, gamma1[...])
+    lower1 = upper1 * scale1 - z1 * dot(lever1.astype(BF16), gamma1[...].astype(BF16))
     grad1 = lower1.astype(BF16).astype(F32)
-    pack_gradients(grads.at[0], x_store, 2, grad1, lever1, z1 * z1, turn)
-    one.step(0)
+    two.step(1)
+    ready = {3: lambda: one.step(0, (0,)), 7: lambda: one.step(0, (1,))}
+    pack_gradients(grads.at[0], x_store, 2, grad1, lever1, z1 * z1, turn, ready)
+    one.step(0, (2, 3))
     one.step(1)
     two.step(2)
     for index in range(2, 7):

time: 61.6 us -> 60 us (0.974)
  Pallas kernels: 60.8 us -> 59.2 us
    pallas_call x1, Pallas kernels: 41.7 us -> 39.6 us  [per_device(): pl.pallas_call(second_kernel, out_shape=shapes, in_specs=[vmem] * 9, out_...]
where the time goes in v7:
time: 60 us; the launch traced here: 59.9 us
  Pallas kernels  59.2 us (99%)
  between operations  0.65 us (1%)
    pallas_call x1, Pallas kernels, per_device(): pl.pallas_call(second_kernel, out_shape=shapes, in_specs=[vmem] * 9, out_...  39.6 us
    pallas_call x1, Pallas kernels, per_device(): pl.pallas_call(first_kernel, out_shape=carried, in_specs=[anywhere] * 8,...  18.1 us
    pallas_call x1, Pallas kernels, per_device(): pl.pallas_call(write_out, out_shape=shapes, in_specs=[vmem] * 7, out_spec...  1.46 us

profile of v7, /device:TPU:1, one launch (start us, length us, event | category | flops | bytes accessed | tf_op | source)
XLA Modules:
  0.0 59.9 jit_solution(10071693803328627154)
XLA Ops:
  0.6 18.1 %shard_map.135 = (f32[26,24,192]{2,1,0:T(8,128)S(1)}, f32[3,30,24,192]{3,2,1,0:T(8,128)S(1)}, f32[3,28,24,192]{3,2,1,0:T(8,128)S(1)}, f32[24,16,192]{2,1,0:T(8,1...) custom-call(bf16[24,16,192]{2,1,0:T(8,128)(2,1)} %x_far.1, ...), custom_call_target="tpu_custom_call" | custom-call | tf_op jit(solution)/shard_map/pallas_call | solution.py:700
  18.8 39.6 %shard_map.136 = (bf16[24,16,192]{2,1,0:T(8,128)(2,1)S(1)}, bf16[9,192,192]{2,1,0:T(8,128)(2,1)S(1)}, f32[192,192]{1,0:T(8,128)S(1)}, f32[1,192]{1,0:T(1,128)S(1...) custom-call(f32[26,24,192]{2,1,0:T(8,128)S(1)} %get-tuple-element.30.cotangent, ...), custom_call_target="tpu_custom_call" | custom-call | tf_op jit(solution)/shard_map/pallas_call | solution.py:730
  58.4 1.5 %shard_map.137 = (bf16[24,16,192]{2,1,0:T(8,128)(2,1)}, bf16[9,192,192]{2,1,0:T(8,128)(2,1)}, f32[192,192]{1,0:T(8,128)}, f32[1,192]{1,0:T(1,128)}, bf16[9,192,1...) custom-call(bf16[24,16,192]{2,1,0:T(8,128)(2,1)S(1)} %get-tuple-element.39.refs_0_, ...), custom_call_target="tpu_custom_call" | custom-call | tf_op jit(solution)/shard_map/pallas_call | solution.py:745

commit v8 on v7

--- a/solution.py
+++ b/solution.py
@@ -392,13 +392,13 @@
     return flat(store[b, start + a : start + a + 24, 0:16]).astype(BF16)
 
 
+def gathered(windows, weight):
+    return dot(jnp.concatenate(windows, axis=1), weight[...].reshape(9 * 192, 192))
+
+
 def outer_convolution(store, weight, rows, ghosts, first, last):
-    total = None
-    for a in range(3):
-        for b in range(3):
-            term = dot(outer_window(store, rows, ghosts, a, b, first, last), weight[3 * a + b])
-            total = term if total is None else total + term
-    return total
+    taps = [(a, b) for a in range(3) for b in range(3)]
+    return gathered([outer_window(store, rows, ghosts, a, b, first, last) for a, b in taps], weight)
 
 
 def place_block(grads, index, value):
@@ -440,13 +440,13 @@
 
 
 def normal_scale(z, gamma, beta):
-    return lax.rsqrt(beta[...] + dot((z * z).astype(BF16), gamma[...].astype(BF16), ((1,), (1,))))
+    return lax.rsqrt(beta[...] + dot((z * z).astype(BF16), gamma[...]))
 
 
 def first_kernel(
     x_far, w1_far, gamma1_far, beta1_far, w2_far, gamma2_far, beta2_far, cot_far,
-    cotangent, x_store, h_store, z_keep, scale_keep, gamma1, w2, gamma2, beta2,
-    x, cot, w1, beta1, field, top_out, bottom_out, west_out, east_out, corner_out, middle_in, corner_in, west_in, east_in, stage, strips,
+    cotangent, x_store, h_store, z_keep, scale_keep, gamma1, w2, gamma2, beta2, w2_turned, gamma2_turned,
+    gamma1_turned, x, cot, w1, beta1, field, top_out, bottom_out, west_out, east_out, corner_out, middle_in, corner_in, west_in, east_in, stage, strips,
     fetched, halo_send, halo_recv,
 ):
     barrier = pltpu.get_barrier_semaphore()
@@ -512,6 +512,10 @@
     cotangent[1:25, 0:16] = cot[...].astype(F32)
     for fetch in fetches[2:]:
         fetch.wait()
+    gamma1_turned[...] = gamma1[...].T.astype(BF16)
+    gamma2_turned[...] = gamma2[...].T.astype(BF16)
+    for tap in range(9):
+        w2_turned[tap] = w2[tap].astype(F32).T.astype(BF16)
 
     copies[0].wait_recv()
     copies[1].wait_recv()
@@ -526,12 +530,8 @@
             target[start : start + 24, 16:24, span] = stage.reshape(24, 8, 128)[:, :, 0:lanes]
 
     def layer(window):
-        z = None
-        for a in range(3):
-            for b in range(3):
-                term = dot(flat(window(a, b)).astype(BF16), w1[3 * a + b])
-                z = term if z is None else z + term
-        scale = normal_scale(z, gamma1, beta1)
+        z = gathered([flat(window(a, b)).astype(BF16) for a in range(3) for b in range(3)], w1)
+        scale = normal_scale(z, gamma1_turned, beta1)
         hidden = (z * scale).astype(BF16).astype(F32)
         return [value.reshape(-1, 24, 192) for value in (z, scale, hidden)]
 
@@ -575,7 +575,7 @@
 
 
 def second_kernel(
-    cotangent, x_store, h_store, z_keep, scale_keep, gamma1, w2, gamma2, beta2,
+    cotangent, x_store, h_store, z_keep, scale_keep, gamma1, w2, gamma2, beta2, w2_turned, gamma2_turned,
     encoded, out_w1, out_g1, out_b1, out_w2, out_g2, out_b2,
     grads, g_store, turn, *scratch,
 ):
@@ -587,7 +587,7 @@
 
     z2 = outer_convolution(h_store, w2, 26, 1, first, last)
     sq2 = z2 * z2
-    scale2 = normal_scale(z2, gamma2, beta2)
+    scale2 = normal_scale(z2, gamma2_turned, beta2)
     encoded[...] = (z2 * scale2).reshape(26, 24, 192)[1:25, 0:16].astype(BF16)
     upper = flat(cotangent[...])
     lever2 = upper * z2 * scale2 * scale2 * scale2
@@ -603,8 +603,8 @@
     pl.semaphore_wait(barrier, len(met))
     two.step(0)
 
-    total = None
     blank = jnp.zeros((1, 16, 192), F32)
+    windows = []
     for a in range(3):
         for b in range(3):
             shifted = g_store.at[2 - b]
@@ -614,13 +614,13 @@
                 window = shifted[1:25, 0:16]
             else:
                 window = jnp.concatenate([blank, shifted[1:24, 0:16]], axis=0)
-            term = dot(flat(window).astype(BF16), w2[3 * a + b], ((1,), (1,)))
-            total = term if total is None else total + term
+            windows.append(flat(window).astype(BF16))
+    total = gathered(windows, w2_turned)
     ghosts = []
     for row, a in ((0, 2 - 2 * first), (25, 2 * last)):
         ghost = None
         for b in range(3):
-            term = dot(g_store[2 - b, row, 0:16].astype(BF16), w2[3 * a + b], ((1,), (1,)))
+            term = dot(g_store[2 - b, row, 0:16].astype(BF16), w2_turned[3 * a + b])
             ghost = term if ghost is None else ghost + term
         ghosts.append(ghost)
     upper1 = jnp.concatenate([total[0:16] + ghosts[0], total[16:368], total[368:384] + ghosts[1]], axis=0)
@@ -695,14 +695,17 @@
             ((9, 192, 192), BF16),
             ((192, 192), F32),
             ((1, 192), F32),
+            ((9, 192, 192), BF16),
+            ((192, 192), BF16),
         )
     ]
     middle = pl.pallas_call(
         first_kernel,
         out_shape=carried,
         in_specs=[anywhere] * 8,
-        out_specs=[vmem] * 9,
+        out_specs=[vmem] * 11,
         scratch_shapes=[
+            pltpu.VMEM((192, 192), BF16),
             pltpu.VMEM((24, 16, 192), BF16),
             pltpu.VMEM((24, 16, 192), BF16),
             pltpu.VMEM((9, 192, 192), BF16),
@@ -730,7 +733,7 @@
     results = pl.pallas_call(
         second_kernel,
         out_shape=shapes,
-        in_specs=[vmem] * 9,
+        in_specs=[vmem] * 11,
         out_specs=[vmem] * 7,
         scratch_shapes=[
             pltpu.VMEM((2, 2, BLOCKS, 128, 128), F32),

time: 60 us -> 59.4 us (0.990)
  Pallas kernels: 59.2 us -> 58.6 us
where the time goes in v8:
time: 59.4 us; the launch traced here: 59.3 us
  Pallas kernels  58.6 us (99%)
  between operations  0.65 us (1%)
    pallas_call x1, Pallas kernels, per_device(): pl.pallas_call(second_kernel, out_shape=shapes, in_specs=[vmem] * 11, out...  39 us
    pallas_call x1, Pallas kernels, per_device(): pl.pallas_call(first_kernel, out_shape=carried, in_specs=[anywhere] * 8,...  18.1 us
    pallas_call x1, Pallas kernels, per_device(): pl.pallas_call(write_out, out_shape=shapes, in_specs=[vmem] * 7, out_spec...  1.46 us

profile of v8, /device:TPU:1, one launch (start us, length us, event | category | flops | bytes accessed | tf_op | source)
XLA Modules:
  0.0 59.3 jit_solution(13219089644030465678)
XLA Ops:
  0.6 18.1 %shard_map.135 = (f32[26,24,192]{2,1,0:T(8,128)S(1)}, f32[3,30,24,192]{3,2,1,0:T(8,128)S(1)}, f32[3,28,24,192]{3,2,1,0:T(8,128)S(1)}, f32[24,16,192]{2,1,0:T(8,1...) custom-call(bf16[24,16,192]{2,1,0:T(8,128)(2,1)} %x_far.1, ...), custom_call_target="tpu_custom_call" | custom-call | tf_op jit(solution)/shard_map/pallas_call | solution.py:702
  18.7 39.0 %shard_map.136 = (bf16[24,16,192]{2,1,0:T(8,128)(2,1)S(1)}, bf16[9,192,192]{2,1,0:T(8,128)(2,1)S(1)}, f32[192,192]{1,0:T(8,128)S(1)}, f32[1,192]{1,0:T(1,128)S(1...) custom-call(f32[26,24,192]{2,1,0:T(8,128)S(1)} %get-tuple-element.32.cotangent, ...), custom_call_target="tpu_custom_call" | custom-call | tf_op jit(solution)/shard_map/pallas_call | solution.py:733
  57.8 1.5 %shard_map.137 = (bf16[24,16,192]{2,1,0:T(8,128)(2,1)}, bf16[9,192,192]{2,1,0:T(8,128)(2,1)}, f32[192,192]{1,0:T(8,128)}, f32[1,192]{1,0:T(1,128)}, bf16[9,192,1...) custom-call(bf16[24,16,192]{2,1,0:T(8,128)(2,1)S(1)} %get-tuple-element.43.refs_0_, ...), custom_call_target="tpu_custom_call" | custom-call | tf_op jit(solution)/shard_map/pallas_call | solution.py:748

commit v9 on v8

--- a/solution.py
+++ b/solution.py
@@ -480,7 +480,9 @@
                 for k, place in enumerate(chosen):
                     rows24 = stage[pl.ds(place - tile, 24, stride=8), :]
                     strips[half, at_row + 24 * k : at_row + 24 * k + 24] = rows24
-        target[...] = strips[...].astype(BF16)
+        target[0:96] = strips[0].astype(BF16)
+        upper = strips[1]
+        target[96:144] = jnp.concatenate([upper[0:48, 0:64], upper[48:96, 0:64]], axis=1).astype(BF16)
 
     strip(west_out, 0, (0, 1, 2), 0)
     strip(east_out, 8, (13, 14, 15), 15)
@@ -523,7 +525,11 @@
         span = slice(128 * half, 128 * half + lanes)
         for target, start, size in ((field, 3, 3), (cotangent, 1, 1)):
             for source, offset in ((east_in, 0), (west_in, 8 - size)):
-                arrived = source[half].astype(F32)
+                if half == 0:
+                    arrived = source[0:96].astype(F32)
+                else:
+                    shared = source[96:144].astype(F32)
+                    arrived = jnp.concatenate([shared, pltpu.roll(shared, 64, axis=1)], axis=0)
                 for k in range(size):
                     at_row = 24 * k if size == 3 else 72
                     stage[pl.ds(offset + k, 24, stride=8), :] = arrived[at_row : at_row + 24]
@@ -713,13 +719,13 @@
             pltpu.VMEM((30, 24, 192), F32),
             pltpu.VMEM((4, 16, 192), BF16),
             pltpu.VMEM((4, 16, 192), BF16),
-            pltpu.VMEM((2, 96, 128), BF16),
-            pltpu.VMEM((2, 96, 128), BF16),
+            pltpu.VMEM((144, 128), BF16),
+            pltpu.VMEM((144, 128), BF16),
             pltpu.VMEM((4, 16, 192), BF16),
             pltpu.VMEM((2, 4, 16, 192), BF16),
             pltpu.VMEM((4, 16, 192), BF16),
-            pltpu.VMEM((2, 96, 128), BF16),
-            pltpu.VMEM((2, 96, 128), BF16),
+            pltpu.VMEM((144, 128), BF16),
+            pltpu.VMEM((144, 128), BF16),
             pltpu.VMEM((192, 128), F32),
             pltpu.VMEM((2, 96, 128), F32),
             pltpu.SemaphoreType.DMA((8,)),

time: 59.4 us -> 59.6 us (level)
  no operation moved by 1% of the time
where the time goes in v9:
time: 59.6 us; the launch traced here: 59.4 us
  Pallas kernels  58.8 us (99%)
  between operations  0.65 us (1%)
    pallas_call x1, Pallas kernels, per_device(): pl.pallas_call(second_kernel, out_shape=shapes, in_specs=[vmem] * 11, out...  39.4 us
    pallas_call x1, Pallas kernels, per_device(): pl.pallas_call(first_kernel, out_shape=carried, in_specs=[anywhere] * 8,...  18 us
    pallas_call x1, Pallas kernels, per_device(): pl.pallas_call(write_out, out_shape=shapes, in_specs=[vmem] * 7, out_spec...  1.46 us

profile of v9, /device:TPU:1, one launch (start us, length us, event | category | flops | bytes accessed | tf_op | source)
XLA Modules:
  0.0 59.4 jit_solution(15232092854347069101)
XLA Ops:
  0.6 18.0 %shard_map.135 = (f32[26,24,192]{2,1,0:T(8,128)S(1)}, f32[3,30,24,192]{3,2,1,0:T(8,128)S(1)}, f32[3,28,24,192]{3,2,1,0:T(8,128)S(1)}, f32[24,16,192]{2,1,0:T(8,1...) custom-call(bf16[24,16,192]{2,1,0:T(8,128)(2,1)} %x_far.1, ...), custom_call_target="tpu_custom_call" | custom-call | tf_op jit(solution)/shard_map/pallas_call | solution.py:708
  18.6 39.4 %shard_map.136 = (bf16[24,16,192]{2,1,0:T(8,128)(2,1)S(1)}, bf16[9,192,192]{2,1,0:T(8,128)(2,1)S(1)}, f32[192,192]{1,0:T(8,128)S(1)}, f32[1,192]{1,0:T(1,128)S(1...) custom-call(f32[26,24,192]{2,1,0:T(8,128)S(1)} %get-tuple-element.32.cotangent, ...), custom_call_target="tpu_custom_call" | custom-call | tf_op jit(solution)/shard_map/pallas_call | solution.py:739
  58.0 1.5 %shard_map.137 = (bf16[24,16,192]{2,1,0:T(8,128)(2,1)}, bf16[9,192,192]{2,1,0:T(8,128)(2,1)}, f32[192,192]{1,0:T(8,128)}, f32[1,192]{1,0:T(1,128)}, bf16[9,192,1...) custom-call(bf16[24,16,192]{2,1,0:T(8,128)(2,1)S(1)} %get-tuple-element.43.refs_0_, ...), custom_call_target="tpu_custom_call" | custom-call | tf_op jit(solution)/shard_map/pallas_call | solution.py:754
